TPU v7x, 512 devices: a whole 4x8x8 slice. The times are simulated.
512 devices in a mesh: leaf: 128 (over z, y, core), sub: 4 (over x).
Axes of the slice: x: 4, y: 8, z: 8, core: 2. Of those that a mesh axis runs over, the one named last changes fastest.
Arguments:
- points: bfloat16 [8192, 64, 256], P(('leaf', 'sub')), may hold values from -6 to 6
- probe_bits: int32 [8192, 16, 256], P(('leaf', 'sub')), may hold values from 0 to 1
- leaf_skel: int32 [8192, 128], P(('leaf', 'sub')), may hold values from 0 to 255, as said below
- leaf_basis: bfloat16 [8192, 128, 256], P(('leaf', 'sub')), may hold values from -0.4375 to 0.4375
- device_skel: int32 [512, 128], P(('leaf', 'sub')), may hold values from 0 to 2047, as said below
- device_basis: bfloat16 [512, 128, 2048], P(('leaf', 'sub')), may hold values from -0.25 to 0.25
- subtree_skel: int32 [128, 128], P('leaf'), may hold values from 0 to 511, as said below
- subtree_basis: bfloat16 [128, 128, 512], P('leaf'), may hold values from -0.375 to 0.375
- upper_skel: int32 [128, 6, 128], P('leaf'), may hold values from 0 to 255, as said below
- upper_basis: bfloat16 [128, 6, 128, 256], P('leaf'), as said below
- near_pairs: int32 [512, 80, 2], P(('leaf', 'sub')), may hold values from 0 to 63, as said below
- near_count: int32 [512], P(('leaf', 'sub')), may hold values from 1 to 80, 16384 in all
- far_pairs: int32 [512, 96, 2], P(('leaf', 'sub')), may hold values from 0 to 63, as said below
Outputs:
- product: float32 [8192, 16, 256], P(('leaf', 'sub'))
Inputs may be any that keep to these rules, and one draw needn't show every extreme that they name: `leaf_skel`: each row names 128 different points of its leaf. `device_skel`: each row names 128 different columns. `subtree_skel`: each row names 128 different columns. `upper_skel`: each row names 128 different columns; entries [g, t-1] are equal for all subtrees g under one node of level t. `upper_basis`: entries [g, t-1] are equal for all subtrees g under one node of level t. `near_pairs`: entry 0 of a row is a leaf of the device (0 to 15), entry 1 a leaf of its subtree numbered 0 to 63 in the subtree, never the first leaf itself; the rows of one device are different pairs. `near_count`: some device has exactly 80 pairs. `far_pairs`: as for near_pairs; every row is used.
All inputs are finite; a program needn't handle non-finite values.
Results may differ from a plain program's by a relative error of at most 0.013.
Values may be sent and summed in bfloat16 or wider, within the bound.
A program may use at most 128 MiB of HBM per device.

v0:
```python
import jax
import jax.numpy as jnp
from jax import lax
from jax.sharding import PartitionSpec as P


def swapped(block, axis, apart):
    count = lax.axis_size(axis)
    route = []
    for low in range(count):
        high = low | 1 << apart
        if high != low and high < count:
            route += [(low, high), (high, low)]
    return lax.ppermute(block, axis, route)


def kernel_tile(first_set, second_set):
    cross_terms = jnp.einsum(
        "...da,...db->...ab", first_set, second_set, preferred_element_type=jnp.float32
    )
    first_wide = first_set.astype(jnp.float32)
    second_wide = second_set.astype(jnp.float32)
    first_norm = jnp.sum(first_wide * first_wide, axis=-2)
    second_norm = jnp.sum(second_wide * second_wide, axis=-2)
    distance = first_norm[..., :, None] + second_norm[..., None, :] - 2.0 * cross_terms
    return jnp.exp(-distance / first_set.shape[-2]).astype(jnp.bfloat16)


def on_device(
    points,
    probe_bits,
    leaf_skel,
    leaf_basis,
    device_skel,
    device_basis,
    subtree_skel,
    subtree_basis,
    upper_skel,
    upper_basis,
    near_pairs,
    near_count,
    far_pairs,
):
    leaves = points.shape[0]
    features = points.shape[1]
    leaf_size = points.shape[2]
    probes = probe_bits.shape[1]
    skeleton = leaf_skel.shape[1]
    groups = lax.axis_size("sub")
    position = lax.axis_index("sub")
    subtree = lax.axis_index("leaf")
    levels = lax.axis_size("leaf").bit_length() - 1
    sign_values = (2 * probe_bits - 1).astype(jnp.bfloat16)
    leaf_coords = jnp.take_along_axis(points, leaf_skel[:, None, :], axis=2)
    leaf_weights = jnp.einsum(
        "lpm,lrm->lpr", sign_values, leaf_basis, preferred_element_type=jnp.float32
    ).astype(jnp.bfloat16)
    joined_weights = jnp.transpose(leaf_weights, (1, 0, 2)).reshape(probes, leaves * skeleton)
    joined_coords = jnp.transpose(leaf_coords, (1, 0, 2)).reshape(features, leaves * skeleton)
    device_weights = jnp.einsum(
        "pc,rc->pr", joined_weights, device_basis[0], preferred_element_type=jnp.float32
    ).astype(jnp.bfloat16)
    device_coords = jnp.take(joined_coords, device_skel[0], axis=1)
    all_points, all_signs, all_coords, all_weights, node_coords, node_weights, all_bases = (
        lax.all_gather(points, "sub", axis=0, tiled=True),
        lax.all_gather(sign_values, "sub", axis=0, tiled=True),
        lax.all_gather(leaf_coords, "sub", axis=0, tiled=True),
        lax.all_gather(leaf_weights, "sub", axis=0, tiled=True),
        lax.all_gather(device_coords[None], "sub", axis=0, tiled=True),
        lax.all_gather(device_weights[None], "sub", axis=0, tiled=True),
        lax.all_gather(leaf_basis, "sub", axis=0, tiled=True),
    )
    self_block = kernel_tile(points, points)
    self_part = jnp.einsum(
        "lpm,lmn->lpn", sign_values, self_block, preferred_element_type=jnp.float32
    )
    group_weights = jnp.transpose(node_weights, (1, 0, 2)).reshape(probes, groups * skeleton)
    group_coords = jnp.transpose(node_coords, (1, 0, 2)).reshape(features, groups * skeleton)
    state_weights = jnp.einsum(
        "pc,rc->pr", group_weights, subtree_basis[0], preferred_element_type=jnp.float32
    ).astype(jnp.bfloat16)
    state_coords = jnp.take(group_coords, subtree_skel[0], axis=1)
    far_own = []
    side_marks = []
    for height in range(1, levels + 1):
        other_coords, other_weights = swapped((state_coords, state_weights), "leaf", height - 1)
        on_right = subtree >> height - 1 & 1 == 1
        left_coords = jnp.where(on_right, other_coords, state_coords)
        right_coords = jnp.where(on_right, state_coords, other_coords)
        left_weights = jnp.where(on_right, other_weights, state_weights)
        right_weights = jnp.where(on_right, state_weights, other_weights)
        kernel_block = kernel_tile(right_coords, left_coords)
        to_left = jnp.dot(right_weights, kernel_block, preferred_element_type=jnp.float32)
        to_right = jnp.einsum(
            "pl,rl->pr", left_weights, kernel_block, preferred_element_type=jnp.float32
        )
        far_own.append(jnp.where(on_right, to_right, to_left))
        side_marks.append(on_right)
        if height < levels:
            both_weights = jnp.concatenate([left_weights, right_weights], axis=1)
            both_coords = jnp.concatenate([left_coords, right_coords], axis=1)
            state_weights = jnp.einsum(
                "pc,rc->pr",
                both_weights,
                upper_basis[0, height - 1],
                preferred_element_type=jnp.float32,
            ).astype(jnp.bfloat16)
            state_coords = jnp.take(both_coords, upper_skel[0, height - 1], axis=1)
    potential = far_own[levels - 1]
    for height in range(levels - 1, 0, -1):
        spread = jnp.dot(
            potential.astype(jnp.bfloat16),
            upper_basis[0, height - 1],
            preferred_element_type=jnp.float32,
        )
        potential = far_own[height - 1] + jnp.where(
            side_marks[height - 1], spread[:, skeleton:], spread[:, :skeleton]
        )
    sub_spread = jnp.dot(
        potential.astype(jnp.bfloat16), subtree_basis[0], preferred_element_type=jnp.float32
    )
    device_potential = lax.dynamic_slice_in_dim(sub_spread, position * skeleton, skeleton, 1)
    dev_spread = jnp.dot(
        device_potential.astype(jnp.bfloat16), device_basis[0], preferred_element_type=jnp.float32
    )
    leaf_potential = jnp.transpose(dev_spread.reshape(probes, leaves, skeleton), (1, 0, 2))
    tree_part = jnp.einsum(
        "lpr,lrm->lpm",
        leaf_potential.astype(jnp.bfloat16),
        leaf_basis,
        preferred_element_type=jnp.float32,
    )
    sub_leaves = all_points.shape[0]
    own_first = position * leaves
    capacity = near_pairs.shape[1]
    first_all = own_first + near_pairs[0, :, 0]
    second_all = near_pairs[0, :, 1]
    first_pair = jnp.int32(0)
    stop_pair = near_count[0]

    def locate(logical):
        return jnp.clip(logical, 0, capacity - 1)

    per_block = min(16, capacity)
    rounds = (jnp.maximum(stop_pair, 0) + per_block - 1) // per_block

    def near_step(counter, partial_value):
        logical = counter * per_block + jnp.arange(per_block, dtype=jnp.int32)
        live_mask = (logical < stop_pair).astype(jnp.float32)[:, None, None]
        slot_ids = locate(logical)
        first_leaf = jnp.take(first_all, slot_ids)
        second_leaf = jnp.take(second_all, slot_ids)
        kernel_block = kernel_tile(
            jnp.take(all_points, second_leaf, axis=0), jnp.take(all_points, first_leaf, axis=0)
        )
        to_first = jnp.einsum(
            "fpm,fmn->fpn",
            jnp.take(all_signs, second_leaf, axis=0),
            kernel_block,
            preferred_element_type=jnp.float32,
        )
        to_second = jnp.einsum(
            "fpn,fmn->fpm",
            jnp.take(all_signs, first_leaf, axis=0),
            kernel_block,
            preferred_element_type=jnp.float32,
        )
        return (
            partial_value.at[first_leaf]
            .add(to_first * live_mask)
            .at[second_leaf]
            .add(to_second * live_mask)
        )

    partial_value = lax.fori_loop(
        0, rounds, near_step, jnp.zeros((sub_leaves, probes, leaf_size), jnp.float32)
    )
    far_first = far_pairs[0, :, 0]
    far_second = far_pairs[0, :, 1]
    far_block = kernel_tile(
        jnp.take(all_coords, far_second, axis=0), jnp.take(leaf_coords, far_first, axis=0)
    )
    to_first_far = jnp.einsum(
        "fpb,fba->fpa",
        jnp.take(all_weights, far_second, axis=0),
        far_block,
        preferred_element_type=jnp.float32,
    ).astype(jnp.bfloat16)
    to_second_far = jnp.einsum(
        "fpa,fba->fpb",
        jnp.take(leaf_weights, far_first, axis=0),
        far_block,
        preferred_element_type=jnp.float32,
    ).astype(jnp.bfloat16)
    first_points = jnp.einsum(
        "fpr,frm->fpm",
        to_first_far,
        jnp.take(leaf_basis, far_first, axis=0),
        preferred_element_type=jnp.float32,
    )
    second_points = jnp.einsum(
        "fpr,frm->fpm",
        to_second_far,
        jnp.take(all_bases, far_second, axis=0),
        preferred_element_type=jnp.float32,
    )
    partial_value = (
        partial_value.at[own_first + far_first].add(first_points).at[far_second].add(second_points)
    )
    mine = lax.psum_scatter(
        partial_value.astype(jnp.bfloat16), "sub", scatter_dimension=0, tiled=True
    ).astype(jnp.float32)
    return mine + self_part + tree_part


def solution(mesh):
    return jax.shard_map(
        on_device,
        mesh=mesh,
        in_specs=(
            P(("leaf", "sub"), None, None),
            P(("leaf", "sub"), None, None),
            P(("leaf", "sub"), None),
            P(("leaf", "sub"), None, None),
            P(("leaf", "sub"), None),
            P(("leaf", "sub"), None, None),
            P("leaf", None),
            P("leaf", None, None),
            P("leaf", None, None),
            P("leaf", None, None, None),
            P(("leaf", "sub"), None, None),
            P(("leaf", "sub")),
            P(("leaf", "sub"), None, None),
        ),
        out_specs=P(("leaf", "sub"), None, None),
        check_vma=False,
    )
```

profile of v0, /device:TPU:8, one launch (start us, length us, event | category | flops | bytes accessed | tf_op | source)
XLA Modules:
  0.0 409.3 jit_solution(4068997933966912420)
XLA Ops:
  9.5 11.1 %gather_fusion.14 = bf16[2048,64]{1,0:T(8,128)(2,1)S(1)} fusion(bf16[16,64,256]{1,2,0:T(8,128)(2,1)S(1)} %copy.26, s32[2048]{0:T(1024)S(1)} %fusion.144), kind=kCustom, calls=%fused_computation.20 | custom fusion | bytes 540672 | tf_op jit(solution)/shard_map/jit(take_along_axis)/gather | solution.py:54
  24.0 12.3 %all-gather = bf16[64,128]{1,0:T(8,128)(2,1)S(1)} all-gather(bf16[16,128]{1,0:T(8,128)(2,1)S(1)} %convolution_convert_fusion.11), channel_id=2, replica_groups=mesh['leaf'=128,'sub'=4] {'sub'}, dimensions={0}, use_global_device_ids=true | all-gather | bytes 20480 | tf_op jit(solution)/shard_map/all_gather | solution.py:70
  39.7 11.9 %all_gather.27 = bf16[4,64,128]{2,1,0:T(8,128)(2,1)S(1)} all-gather(bf16[1,64,128]{2,1,0:T(8,128)(2,1)S(1)} %copy.32), channel_id=1, replica_groups=mesh['leaf'=128,'sub'=4] {'sub'}, dimensions={0}, use_global_device_ids=true | all-gather | bytes 81920 | tf_op jit(solution)/shard_map/all_gather | solution.py:69
  55.2 13.7 %all_gather.21 = bf16[64,16,256]{2,1,0:T(8,128)(2,1)} all-gather(bf16[16,16,256]{2,1,0:T(8,128)(2,1)S(1)} %add_convert_fusion), channel_id=1, replica_groups=mesh['leaf'=128,'sub'=4] {'sub'}, dimensions={0}, use_global_device_ids=true | all-gather | bytes 655360 | tf_op jit(solution)/shard_map/all_gather | solution.py:66
  78.5 7.8 %collective-permute-start.2 = (bf16[16,128]{1,0:T(8,128)(2,1)S(1)}, bf16[16,128]{1,0:T(8,128)(2,1)S(1)}, u32[]{:S(2)}, u32[]{:S(2)}) collective-permute-start(bf16[16,128]{1,0:T(8,128)(2,1)S(1)} %convolution_convert_fusion.9), channel_id=1, source_target_pairs={{0,8},{8,0},{4,12},{12,4},{16,24},{24,16},{20,28},{28,20},{32,40},... | collective-permute-start | bytes 12296 | tf_op jit(solution)/shard_map/ppermute | solution.py:14
  91.1 3.9 collective-permute-done.4
  95.7 3.0 collective-permute-start.6
  98.7 12.6 %all_gather.23 = bf16[64,16,128]{2,1,0:T(8,128)(2,1)S(1)} all-gather(bf16[16,16,128]{2,1,0:T(8,128)(2,1)S(1)} %convolution_convert_fusion.2), channel_id=1, replica_groups=mesh['leaf'=128,'sub'=4] {'sub'}, dimensions={0}, use_global_device_ids=true | all-gather | bytes 327680 | tf_op jit(solution)/shard_map/all_gather | solution.py:68
  112.0 6.1 %gather_fusion.9 = bf16[96,128,256]{2,1,0:T(8,128)(2,1)} fusion(bf16[16,128,256]{2,1,0:T(8,128)(2,1)S(1)} %copy-done.1, s32[1024]{0:T(1024)} %copy-done.50), kind=kCustom, calls=%fused_computation.15 | custom fusion | bytes 12583296 | tf_op jit(solution)/shard_map/jit(_take)/gather | solution.py:198
  124.0 4.0 collective-permute-start.8
  130.9 6.2 %collective-permute-start.10 = (bf16[16,128]{1,0:T(8,128)(2,1)S(1)}, bf16[16,128]{1,0:T(8,128)(2,1)S(1)}, u32[]{:S(2)}, u32[]{:S(2)}) collective-permute-start(bf16[16,128]{1,0:T(8,128)(2,1)S(1)} %convolution_convert_fusion.5), channel_id=1, source_target_pairs={{0,128},{128,0},{4,132},{132,4},{8,136},{136,8},{12,140},{140,12},... | collective-permute-start | bytes 12296 | tf_op jit(solution)/shard_map/ppermute | solution.py:14
  138.5 3.3 collective-permute-start.3
  142.0 8.7 %collective-permute-start.12 = (bf16[16,128]{1,0:T(8,128)(2,1)S(1)}, bf16[16,128]{1,0:T(8,128)(2,1)S(1)}, u32[]{:S(2)}, u32[]{:S(2)}) collective-permute-start(bf16[16,128]{1,0:T(8,128)(2,1)S(1)} %convolution_convert_fusion.4), channel_id=1, source_target_pairs={{0,256},{256,0},{4,260},{260,4},{8,264},{264,8},{12,268},{268,12},... | collective-permute-start | bytes 12296 | tf_op jit(solution)/shard_map/ppermute | solution.py:14
  156.5 3.4 collective-permute-done.5
  165.1 6.9 %collective-permute-done.7 = bf16[64,128]{0,1:T(8,128)(2,1)S(1)} collective-permute-done((bf16[64,128]{0,1:T(8,128)(2,1)S(1)}, bf16[64,128]{0,1:T(8,128)(2,1)S(1)}, u32[]{:S(2)}, u32[]{:S(2)}) %collective-permute-start.7) | collective-permute-done | bytes 16416 | tf_op jit(solution)/shard_map/ppermute | solution.py:14
  174.3 2.7 collective-permute-start.9
  185.7 3.9 collective-permute-done.11
  192.1 2.6 collective-permute-start.13
  195.0 6.8 %collective-permute-done.13 = bf16[64,128]{0,1:T(8,128)(2,1)S(1)} collective-permute-done((bf16[64,128]{0,1:T(8,128)(2,1)S(1)}, bf16[64,128]{0,1:T(8,128)(2,1)S(1)}, u32[]{:S(2)}, u32[]{:S(2)}) %collective-permute-start.13) | collective-permute-done | bytes 16416 | tf_op jit(solution)/shard_map/ppermute | solution.py:14
  204.1 3.3 gather_fusion.7
  209.4 6.1 %exponential_convert_fusion.1 = bf16[96,128,128]{2,1,0:T(8,128)(2,1)} fusion(f32[96,128]{1,0:T(8,128)S(1)} %copy-done.31, f32[96,128]{1,0:T(8,128)S(1)} %multiply_reduce_fusion.3, bf16[96,64,128]{2,1,0:T(8,128)(2,1)} %gather_fusion.7, pred[96]{0:T(512)(128)(4,1)S(1)} %copy-done.55, bf16[96,64,128]{2,1,0:T(8,128)(2,1)S(1)} %gather_fusion.8, ...), kind=kOutput, calls=%fused_computation.56 | convolution fusion | flops 212336640 | bytes 6389952 | tf_op jit(solution)/shard_map/...da,...db->...ab/dot_general | solution.py:18
  215.5 6.7 %fusion.11 = f32[96,16,256]{2,1,0:T(8,128)} fusion(bf16[96,128,256]{2,1,0:T(8,128)(2,1)} %gather_fusion.9, pred[96]{0:T(512)(128)(4,1)S(1)} %copy-done.57, bf16[96,128,128]{2,1,0:T(8,128)(2,1)} %exponential_convert_fusion.1, bf16[96,16,128]{2,1,0:T(8,128)(2,1)S(1)} %copy-done.15, pred[96]{0:T(512)(128)(4,1)S(1)} %copy-done.55), kind=kOutput, calls=%fused_computation.54 | convolution fusion | flops 154533888 | bytes 11403456 | tf_op jit(solution)/shard_map/fpr,frm->fpm/dot_general | solution.py:195
  223.3 47.1 %while.10 = (s32[]{:T(128)}, f32[64,16,256]{2,1,0:T(8,128)}, s32[]{:T(128)}, s32[80]{0:T(128)S(1)}, s32[80]{0:T(128)S(1)}, /*index=5*/bf16[64,16,256]{2,1,0:T(8,...) while((s32[]{:T(128)}, f32[64,16,256]{2,1,0:T(8,128)}, s32[]{:T(128)}, ...), condition=%wide.region_5.9_spmd, body=%wide.region_0.8_spmd.sunk | while | flops 210628064 | bytes 17644208 | solution.py:175
  230.4 2.7 exponential_convert_fusion.4
  237.9 2.6 scatter_fusion
  254.0 2.7 exponential_convert_fusion.4
  261.5 2.6 scatter_fusion
  270.5 13.3 %scatter_fusion.2 = f32[64,16,256]{2,1,0:T(8,128)} fusion(f32[64,16,256]{2,1,0:T(8,128)} %get-tuple-element.52, s32[96]{0:T(128)} %get-tuple-element.153, f32[96,16,256]{2,1,0:T(8,128)} %fusion.11), kind=kCustom, calls=%fused_computation.23 | custom fusion | flops 393216 | bytes 4718976 | tf_op jit(solution)/shard_map/scatter-add | solution.py:208
  283.8 8.3 %gather_fusion.11 = bf16[96,128,256]{2,1,0:T(8,128)(2,1)} fusion(bf16[64,128,256]{2,1,0:T(8,128)(2,1)} %all-gather.9.cloned.1.call-done, s32[1024]{0:T(1024)} %get-tuple-element.157), kind=kCustom, calls=%fused_computation.17 | custom fusion | bytes 12583296 | tf_op jit(solution)/shard_map/jit(_take)/gather | solution.py:204
  292.2 7.6 %fusion.9 = f32[96,16,256]{2,1,0:T(8,128)} fusion(bf16[96,128,256]{2,1,0:T(8,128)(2,1)} %gather_fusion.11, pred[96]{0:T(512)(128)(4,1)S(1)} %copy-done.56, bf16[96,128,128]{2,1,0:T(8,128)(2,1)} %exponential_convert_fusion.1, bf16[96,16,128]{2,1,0:T(8,128)(2,1)S(1)} %copy-done.14, pred[96]{0:T(512)(128)(4,1)S(1)} %copy-done.58), kind=kOutput, calls=%fused_computation.52 | convolution fusion | flops 154533888 | bytes 11403456 | tf_op jit(solution)/shard_map/fpr,frm->fpm/dot_general | solution.py:201
  300.0 8.9 %scatter_fusion.3 = f32[64,16,256]{2,1,0:T(8,128)S(1)} fusion(f32[64,16,256]{2,1,0:T(8,128)S(1)} %copy-done.2, s32[96]{0:T(128)S(1)} %copy-done.52, f32[96,16,256]{2,1,0:T(8,128)} %fusion.9), kind=kCustom, calls=%fused_computation.24 | custom fusion | flops 393216 | bytes 4718976 | tf_op jit(solution)/shard_map/scatter-add | solution.py:208
  311.2 88.0 %reduce-scatter.2.cloned.1.call-done = bf16[16,16,256]{2,1,0:T(8,128)(2,1)} async-done(((bf16[64,16,256]{2,1,0:T(8,128)(2,1)}), bf16[16,16,256]{2,1,0:T(8,128)(2,1)}) %reduce-scatter.2.cloned.1.call-update) | async-done | bytes 131088 | tf_op jit(solution)/shard_map/reduce_scatter | solution.py:210
  (299 shorter events, 110.5 us)
Async XLA Ops:
  6.5 29.8 %copy-start = (bf16[1,128,512]{2,1,0:T(8,128)(2,1)S(1)}, bf16[1,128,512]{2,1,0:T(8,128)(2,1)}, u32[]{:S(2)}) copy-start(bf16[1,128,512]{2,1,0:T(8,128)(2,1)} %param.30) | copy-start | bytes 393220
  6.5 197.5 %all-gather.7.cloned.1.call-start = ((), (), s32[]{:S(2)}) async-start(), calls=%async_computation.2 | async-start | bytes 1310720 | tf_op jit(solution)/shard_map/all_gather | solution.py:67
  20.9 33.5 %copy-start.6 = (bf16[16,64,256]{2,1,0:T(8,128)(2,1)S(1)}, bf16[16,64,256]{2,1,0:T(8,128)(2,1)}, u32[]{:S(2)}) copy-start(bf16[16,64,256]{2,1,0:T(8,128)(2,1)} %param.23) | copy-start | bytes 1572868
  21.7 200.5 %all-gather.5.cloned.1.call-start = ((), (), s32[]{:S(2)}) async-start(), calls=%async_computation.1 | async-start | bytes 2621440 | tf_op jit(solution)/shard_map/all_gather | solution.py:65
  22.5 46.4 %copy-start.53 = (s32[1,96,2]{1,2,0:T(2,128)S(1)}, s32[1,96,2]{1,2,0:T(2,128)}, u32[]{:S(2)}) copy-start(s32[1,96,2]{1,2,0:T(2,128)} %param.35) | copy-start | bytes 2308
  22.5 47.5 %copy-start.59 = (s32[1,80,2]{1,2,0:T(2,128)S(1)}, s32[1,80,2]{1,2,0:T(2,128)}, u32[]{:S(2)}) copy-start(s32[1,80,2]{1,2,0:T(2,128)} %param.33) | copy-start | bytes 1924
  22.5 48.1 %copy-start.5 = (bf16[16,64,128]{2,1,0:T(8,128)(2,1)S(1)}, bf16[16,64,128]{2,1,0:T(8,128)(2,1)}, u32[]{:S(2)}) copy-start(bf16[16,64,128]{2,1,0:T(8,128)(2,1)} %get-tuple-element.114) | copy-start | bytes 786436
  22.5 261.3 %all-gather.9.cloned.1.call-start = ((), (), s32[]{:S(2)}) async-start(), calls=%async_computation.3 | async-start | bytes 5242880 | tf_op jit(solution)/shard_map/all_gather | solution.py:71
  23.2 375.9 %reduce-scatter.2.cloned.1.call-start = ((), (), s32[]{:S(2)}) async-start(), calls=%async_computation.4 | async-start | bytes 655360 | tf_op jit(solution)/shard_map/reduce_scatter | solution.py:210
  23.3 47.3 %copy-start.10 = (bf16[16,16,256]{2,1,0:T(8,128)(2,1)}, bf16[16,16,256]{2,1,0:T(8,128)(2,1)S(1)}, u32[]{:S(2)}) copy-start(bf16[16,16,256]{2,1,0:T(8,128)(2,1)S(1)} %add_convert_fusion) | copy-start | bytes 393220
  36.4 40.6 %collective-permute-start = (bf16[16,128]{1,0:T(8,128)(2,1)S(1)}, bf16[16,128]{1,0:T(8,128)(2,1)}, u32[]{:S(2)}, u32[]{:S(2)}) collective-permute-start(bf16[16,128]{1,0:T(8,128)(2,1)S(1)} %convolution_convert_fusion.10), channel_id=1, source_target_pairs={{0,4},{4,0},{8,12},{12,8},{16,20},{20,16},{24,28},{28,24},{32,36},... | collective-permute-start | bytes 12296 | tf_op jit(solution)/shard_map/ppermute | solution.py:14
  38.4 32.2 %copy-start.54 = (pred[128]{0:T(512)(128)(4,1)}, pred[128]{0:T(512)(128)(4,1)S(1)}, u32[]{:S(2)}) copy-start(pred[128]{0:T(512)(128)(4,1)S(1)} %compare_and_fusion.11) | copy-start | bytes 388
  52.5 75.5 %collective-permute-start.1 = (bf16[64,128]{0,1:T(8,128)(2,1)S(1)}, bf16[64,128]{0,1:T(8,128)(2,1)}, u32[]{:S(2)}, u32[]{:S(2)}) collective-permute-start(bf16[64,128]{0,1:T(8,128)(2,1)S(1)} %select_bitcast_fusion.6), channel_id=1, source_target_pairs={{0,4},{4,0},{8,12},{12,8},{16,20},{20,16},{24,28},{28,24},{32,36},... | collective-permute-start | bytes 49160 | tf_op jit(solution)/shard_map/ppermute | solution.py:14
  78.5 9.4 %collective-permute-start.2 = (bf16[16,128]{1,0:T(8,128)(2,1)S(1)}, bf16[16,128]{1,0:T(8,128)(2,1)S(1)}, u32[]{:S(2)}, u32[]{:S(2)}) collective-permute-start(bf16[16,128]{1,0:T(8,128)(2,1)S(1)} %convolution_convert_fusion.9), channel_id=1, source_target_pairs={{0,8},{8,0},{4,12},{12,4},{16,24},{24,16},{20,28},{28,20},{32,40},... | collective-permute-start | bytes 12296 | tf_op jit(solution)/shard_map/ppermute | solution.py:14
  88.5 6.4 %collective-permute-start.4 = (bf16[16,128]{1,0:T(8,128)(2,1)S(1)}, bf16[16,128]{1,0:T(8,128)(2,1)S(1)}, u32[]{:S(2)}, u32[]{:S(2)}) collective-permute-start(bf16[16,128]{1,0:T(8,128)(2,1)S(1)} %convolution_convert_fusion.8), channel_id=1, source_target_pairs={{0,16},{16,0},{4,20},{20,4},{8,24},{24,8},{12,28},{28,12},{32,48},... | collective-permute-start | bytes 12296 | tf_op jit(solution)/shard_map/ppermute | solution.py:14
  95.7 27.4 %collective-permute-start.6 = (bf16[16,128]{1,0:T(8,128)(2,1)}, bf16[16,128]{1,0:T(8,128)(2,1)}, u32[]{:S(2)}, u32[]{:S(2)}) collective-permute-start(bf16[16,128]{1,0:T(8,128)(2,1)} %convolution_convert_fusion.7), channel_id=1, source_target_pairs={{0,32},{32,0},{4,36},{36,4},{8,40},{40,8},{12,44},{44,12},{16,48},... | collective-permute-start | bytes 12296 | tf_op jit(solution)/shard_map/ppermute | solution.py:14
  124.0 6.8 %collective-permute-start.8 = (bf16[16,128]{1,0:T(8,128)(2,1)S(1)}, bf16[16,128]{1,0:T(8,128)(2,1)S(1)}, u32[]{:S(2)}, u32[]{:S(2)}) collective-permute-start(bf16[16,128]{1,0:T(8,128)(2,1)S(1)} %convolution_convert_fusion.6), channel_id=1, source_target_pairs={{0,64},{64,0},{4,68},{68,4},{8,72},{72,8},{12,76},{76,12},{16,80},... | collective-permute-start | bytes 12296 | tf_op jit(solution)/shard_map/ppermute | solution.py:14
  129.1 78.2 %copy-start.17 = (bf16[128,128]{1,0:T(8,128)(2,1)}, bf16[128,128]{1,0:T(8,128)(2,1)S(1)}, u32[]{:S(2)}) copy-start(bf16[128,128]{1,0:T(8,128)(2,1)S(1)} %fusion.48) | copy-start | bytes 98308
  130.9 10.9 %collective-permute-start.10 = (bf16[16,128]{1,0:T(8,128)(2,1)S(1)}, bf16[16,128]{1,0:T(8,128)(2,1)S(1)}, u32[]{:S(2)}, u32[]{:S(2)}) collective-permute-start(bf16[16,128]{1,0:T(8,128)(2,1)S(1)} %convolution_convert_fusion.5), channel_id=1, source_target_pairs={{0,128},{128,0},{4,132},{132,4},{8,136},{136,8},{12,140},{140,12},... | collective-permute-start | bytes 12296 | tf_op jit(solution)/shard_map/ppermute | solution.py:14
  138.5 12.2 %collective-permute-start.3 = (bf16[64,128]{0,1:T(8,128)(2,1)S(1)}, bf16[64,128]{0,1:T(8,128)(2,1)S(1)}, u32[]{:S(2)}, u32[]{:S(2)}) collective-permute-start(bf16[64,128]{0,1:T(8,128)(2,1)S(1)} %select_bitcast_fusion.5), channel_id=1, source_target_pairs={{0,8},{8,0},{4,12},{12,4},{16,24},{24,16},{20,28},{28,20},{32,40},... | collective-permute-start | bytes 49160 | tf_op jit(solution)/shard_map/ppermute | solution.py:14
  142.0 60.8 %collective-permute-start.12 = (bf16[16,128]{1,0:T(8,128)(2,1)S(1)}, bf16[16,128]{1,0:T(8,128)(2,1)S(1)}, u32[]{:S(2)}, u32[]{:S(2)}) collective-permute-start(bf16[16,128]{1,0:T(8,128)(2,1)S(1)} %convolution_convert_fusion.4), channel_id=1, source_target_pairs={{0,256},{256,0},{4,260},{260,4},{8,264},{264,8},{12,268},{268,12},... | collective-permute-start | bytes 12296 | tf_op jit(solution)/shard_map/ppermute | solution.py:14
  153.1 6.7 %collective-permute-start.5 = (bf16[64,128]{0,1:T(8,128)(2,1)S(1)}, bf16[64,128]{0,1:T(8,128)(2,1)S(1)}, u32[]{:S(2)}, u32[]{:S(2)}) collective-permute-start(bf16[64,128]{0,1:T(8,128)(2,1)S(1)} %select_bitcast_fusion.4), channel_id=1, source_target_pairs={{0,16},{16,0},{4,20},{20,4},{8,24},{24,8},{12,28},{28,12},{32,48},... | collective-permute-start | bytes 49160 | tf_op jit(solution)/shard_map/ppermute | solution.py:14
  160.6 46.7 %copy-start.55 = (pred[96]{0:T(512)(128)(4,1)S(1)}, pred[96]{0:T(512)(128)(4,1)}, u32[]{:S(2)}) copy-start(pred[96]{0:T(512)(128)(4,1)} %get-tuple-element.149) | copy-start | bytes 292
  162.2 9.7 %collective-permute-start.7 = (bf16[64,128]{0,1:T(8,128)(2,1)S(1)}, bf16[64,128]{0,1:T(8,128)(2,1)S(1)}, u32[]{:S(2)}, u32[]{:S(2)}) collective-permute-start(bf16[64,128]{0,1:T(8,128)(2,1)S(1)} %select_bitcast_fusion.3), channel_id=1, source_target_pairs={{0,32},{32,0},{4,36},{36,4},{8,40},{40,8},{12,44},{44,12},{16,48},... | collective-permute-start | bytes 49160 | tf_op jit(solution)/shard_map/ppermute | solution.py:14
  174.3 5.8 %collective-permute-start.9 = (bf16[64,128]{0,1:T(8,128)(2,1)S(1)}, bf16[64,128]{0,1:T(8,128)(2,1)S(1)}, u32[]{:S(2)}, u32[]{:S(2)}) collective-permute-start(bf16[64,128]{0,1:T(8,128)(2,1)S(1)} %select_bitcast_fusion.2), channel_id=1, source_target_pairs={{0,64},{64,0},{4,68},{68,4},{8,72},{72,8},{12,76},{76,12},{16,80},... | collective-permute-start | bytes 49160 | tf_op jit(solution)/shard_map/ppermute | solution.py:14
  182.5 26.8 %copy-start.31 = (f32[96,128]{1,0:T(8,128)S(1)}, f32[96,128]{1,0:T(8,128)}, u32[]{:S(2)}) copy-start(f32[96,128]{1,0:T(8,128)} %multiply_reduce_fusion.2) | copy-start | bytes 147460
  182.6 7.1 %collective-permute-start.11 = (bf16[64,128]{0,1:T(8,128)(2,1)S(1)}, bf16[64,128]{0,1:T(8,128)(2,1)S(1)}, u32[]{:S(2)}, u32[]{:S(2)}) collective-permute-start(bf16[64,128]{0,1:T(8,128)(2,1)S(1)} %select_bitcast_fusion.1), channel_id=1, source_target_pairs={{0,128},{128,0},{4,132},{132,4},{8,136},{136,8},{12,140},{140,12},... | collective-permute-start | bytes 49160 | tf_op jit(solution)/shard_map/ppermute | solution.py:14
  192.1 9.7 %collective-permute-start.13 = (bf16[64,128]{0,1:T(8,128)(2,1)S(1)}, bf16[64,128]{0,1:T(8,128)(2,1)S(1)}, u32[]{:S(2)}, u32[]{:S(2)}) collective-permute-start(bf16[64,128]{0,1:T(8,128)(2,1)S(1)} %select_bitcast_fusion), channel_id=1, source_target_pairs={{0,256},{256,0},{4,260},{260,4},{8,264},{264,8},{12,268},{268,12},... | collective-permute-start | bytes 49160 | tf_op jit(solution)/shard_map/ppermute | solution.py:14
  299.9 99.2 %copy-start.7 = (bf16[16,64,256]{2,1,0:T(8,128)(2,1)S(1)}, bf16[16,64,256]{2,1,0:T(8,128)(2,1)}, u32[]{:S(2)}) copy-start(bf16[16,64,256]{2,1,0:T(8,128)(2,1)} %param.23) | copy-start | bytes 1572868
  299.9 99.2 %copy-start.11 = (bf16[16,16,256]{2,1,0:T(8,128)(2,1)S(1)}, bf16[16,16,256]{2,1,0:T(8,128)(2,1)}, u32[]{:S(2)}) copy-start(bf16[16,16,256]{2,1,0:T(8,128)(2,1)} %copy-done.10) | copy-start | bytes 393220
  300.0 99.2 %copy-start.38 = (f32[16,256]{1,0:T(8,128)S(1)}, f32[16,256]{1,0:T(8,128)}, u32[]{:S(2)}) copy-start(f32[16,256]{1,0:T(8,128)} %multiply_reduce_fusion.4) | copy-start | bytes 49156
  311.2 90.4 %copy-start.8 = (bf16[2048,128]{1,0:T(8,128)(2,1)S(1)}, bf16[2048,128]{1,0:T(8,128)(2,1)}, u32[]{:S(2)}) copy-start(bf16[2048,128]{1,0:T(8,128)(2,1)} %copy.36) | copy-start | bytes 1572868
  (54 other events, 468.6 us)
Sparse Core Ops, SparseCore 0:
  21.8 33.8 all-gather.6
  57.9 36.8 all-gather.4
  96.8 53.6 all-gather.8
  309.9 89.2 reduce-scatter.1
where the time goes:
time: 413 us; the launch traced here: 409 us
  waiting for transfers between devices  117 us (28%)
  local copies, waits for them, and re-layouts  69.1 us (17%)
  other arithmetic  61 us (15%)
  starting transfers between devices  50.7 us (12%)
  blocking collectives  50.5 us (12%)
  matrix products  45.4 us (11%)
  between operations  14.9 us (4%)
    reduce_scatter x1, waiting for transfers between devices, on_device(): lax.psum_scatter(partial_value.astype(jnp.bfloat16), 'sub', scatter_dimen...  88 us
    ppermute x14, starting transfers between devices, swapped(): return lax.ppermute(block, axis, route)  50.6 us
    ppermute x14, waiting for transfers between devices, swapped(): return lax.ppermute(block, axis, route)  28.1 us
    scatter-add x2, other arithmetic, on_device(): partial_value.at[own_first + far_first].add(first_points).at[far_second]  22.2 us
    all_gather x1, blocking collectives, on_device(): lax.all_gather(sign_values, 'sub', axis=0, tiled=True)  13.7 us
    dot_general x10, matrix products, kernel_tile(): jnp.einsum('...da,...db->...ab', first_set, second_set, preferred_element...  12.7 us
    all_gather x1, blocking collectives, on_device(): lax.all_gather(leaf_weights, 'sub', axis=0, tiled=True)  12.6 us
    all_gather x1, blocking collectives, on_device(): lax.all_gather(device_weights[None], 'sub', axis=0, tiled=True)  12.3 us
  transfers between devices with their start and end apart: 18, of which 8 were waited for; matrix products, arithmetic and copies ran while one was open for 31% of the time, Pallas kernels for 0%

commit v1 on v0

v1 whole, which is shorter than its diff:
```python
import functools
import math

import jax
import jax.numpy as jnp
from jax import lax
from jax.experimental import pallas as pl
from jax.experimental.pallas import tpu as pltpu
from jax.sharding import PartitionSpec as P

F32 = jnp.float32
BF = jnp.bfloat16
I32 = jnp.int32
MESH = pl.DeviceIdType.MESH
VM = pl.BlockSpec(memory_space=pltpu.VMEM)
SM = pl.BlockSpec(memory_space=pltpu.SMEM)
NEAR_GROUP = 4
FAR_GROUP = 8
QUEUE = 256


def dot(a, b, ca=1, cb=0):
    return lax.dot_general(a, b, (((ca,), (cb,)), ((), ())), preferred_element_type=F32)


def one_hot(rows, row):
    spot = lax.broadcasted_iota(I32, (rows, row.shape[1]), 0) == row
    return jnp.where(spot, 1.0, 0.0).astype(BF)


def norm_parts(coords):
    wide = coords.astype(F32)
    norm = jnp.sum(wide * wide, axis=0, keepdims=True)
    high = norm.astype(BF).astype(F32)
    rest = norm - high
    middle = rest.astype(BF).astype(F32)
    return -high, -middle, middle - rest


def row_form(coords, parts):
    high, middle, low = parts
    at = lax.broadcasted_iota(I32, (16, coords.shape[1]), 0)
    tail = jnp.where(
        at < 3, 1.0, jnp.where(at == 3, high, jnp.where(at == 4, middle, jnp.where(at == 5, low, 0.0)))
    )
    return jnp.concatenate(
        [coords, tail.astype(BF), jnp.zeros((48, coords.shape[1]), BF)], axis=0
    )


def column_form(coords, parts):
    high, middle, low = parts
    at = lax.broadcasted_iota(I32, (16, coords.shape[1]), 0)
    tail = jnp.where(
        at == 0, high, jnp.where(at == 1, middle, jnp.where(at == 2, low, jnp.where(at < 6, 1.0, 0.0)))
    )
    return jnp.concatenate(
        [coords + coords, tail.astype(BF), jnp.zeros((48, coords.shape[1]), BF)], axis=0
    )


def tile(columns, rows, scale):
    return jnp.exp2(dot(columns, rows) * scale).astype(BF)


def upward_kernel(
    levels,
    points,
    bits,
    leaf_skel,
    leaf_basis,
    device_skel,
    device_basis,
    subtree_skel,
    subtree_basis,
    upper_skel,
    upper_basis,
    near_pairs,
    near_count,
    far_pairs,
    leaf_columns,
    leaf_rows,
    skel_columns,
    skel_rows,
    signs,
    weights,
    self_part,
    far_own,
    near_queue,
    far_queue,
    far_points,
    far_skel,
    joined,
    nodes,
    states,
    lists,
    tiles,
    near_packed,
    far_packed,
    send_sem,
    recv_sem,
    pass_sem,
    node_send,
    node_recv,
    state_send,
    state_recv,
    queue_sem,
):
    leaves, features, size = points.shape
    scale = math.log2(math.e) / features
    place = lax.axis_index("sub")
    tree = lax.axis_index("leaf")
    odd = tree & 1
    behind = (place + 3 - 2 * odd) & 3
    partners = [tree ^ (1 << t) for t in range(levels)]

    barrier = pltpu.get_barrier_semaphore()
    for k in range(1, 4):
        pl.semaphore_signal(barrier, inc=1, device_id={"sub": (place + k) & 3}, device_id_type=MESH)
    for partner in partners:
        pl.semaphore_signal(barrier, inc=1, device_id={"leaf": partner}, device_id_type=MESH)

    def make_signs(leaf, _):
        signs[leaf] = (2 * bits[leaf] - 1).astype(F32).astype(BF)
        return 0

    lax.fori_loop(0, leaves, make_signs, 0, unroll=4)
    own_list = jnp.zeros((8, 128), I32)
    lists[0] = own_list
    near_t = jnp.transpose(near_pairs[0])
    far_t = jnp.transpose(far_pairs[0])
    lists[0, 0:2, 0 : near_t.shape[1]] = near_t
    lists[0, 2:4, 0 : far_t.shape[1]] = far_t
    lists[0, 4:5, :] = jnp.full((1, 128), near_count[0], I32)

    pl.semaphore_wait(barrier, 3 + levels)

    quarter = leaves // 4

    def own_copy(k):
        if k < 4:
            part = pl.ds(k * quarter, quarter)
            pair = (points.at[part], far_points.at[0, part])
        elif k == 4:
            pair = (signs.at[pl.ds(0, leaves)], signs.at[pl.ds(leaves, leaves)])
        elif k == 5:
            pair = (leaf_skel, far_skel.at[0])
        elif k == 6:
            pair = (lists.at[0], lists.at[1])
        else:
            pair = (weights.at[pl.ds(0, leaves)], weights.at[pl.ds(leaves, leaves)])
        return pltpu.make_async_remote_copy(
            src_ref=pair[0],
            dst_ref=pair[1],
            send_sem=send_sem.at[k],
            recv_sem=recv_sem.at[k],
            device_id={"sub": behind},
            device_id_type=MESH,
        )

    def passed_copy(k):
        if k < 4:
            part = pl.ds(k * quarter, quarter)
            pair = (far_points.at[0, part], far_points.at[1, part])
        elif k == 4:
            pair = (signs.at[pl.ds(leaves, leaves)], signs.at[pl.ds(2 * leaves, leaves)])
        elif k == 5:
            pair = (far_skel.at[0], far_skel.at[1])
        else:
            pair = (weights.at[pl.ds(leaves, leaves)], weights.at[pl.ds(2 * leaves, leaves)])
        return pltpu.make_async_remote_copy(
            src_ref=pair[0],
            dst_ref=pair[1],
            send_sem=send_sem.at[8 + k],
            recv_sem=pass_sem.at[k],
            device_id={"sub": behind},
            device_id_type=MESH,
        )

    for k in (5, 6, 0, 1, 2, 3, 4):
        own_copy(k).start()

    def leaf_step(leaf, _):
        coords = points[leaf]
        parts = norm_parts(coords)
        rows = row_form(coords, parts)
        leaf_rows[leaf] = rows
        picked = dot(rows, one_hot(size, leaf_skel[pl.ds(leaf, 1), :])).astype(BF)
        skel_rows[leaf] = picked
        lane = pl.ds(pl.multiple_of(leaf * 128, 128), 128)
        joined[0:features, lane] = picked[0:features]
        weight = dot(signs[leaf], leaf_basis[leaf], 1, 1).astype(BF)
        weights[leaf] = weight
        joined[features : features + 16, lane] = weight
        return 0

    lax.fori_loop(0, leaves, leaf_step, 0, unroll=4)
    own_copy(7).start()
    nodes[place, 0:features] = dot(
        joined[0:features], one_hot(joined.shape[1], device_skel[...])
    ).astype(BF)
    nodes[place, features:] = dot(joined[features:], device_basis[0], 1, 1).astype(BF)

    def node_copy(k):
        return pltpu.make_async_remote_copy(
            src_ref=nodes.at[place],
            dst_ref=nodes.at[place],
            send_sem=node_send.at[k - 1],
            recv_sem=node_recv.at[k - 1],
            device_id={"sub": (place + k) & 3},
            device_id_type=MESH,
        )

    for k in range(1, 4):
        node_copy(k).start()

    def own_columns(leaf, _):
        coords = points[leaf]
        columns = column_form(coords, norm_parts(coords))
        leaf_columns[leaf] = jnp.transpose(columns)
        coords = skel_rows[leaf, 0:features]
        skel_columns[leaf] = jnp.transpose(column_form(coords, norm_parts(coords)))
        return 0

    def passed_columns(slot, leaf):
        columns = column_form(far_points[slot, leaf], norm_parts(far_points[slot, leaf]))
        leaf_columns[(slot + 1) * leaves + leaf] = jnp.transpose(columns)
        picked = dot(columns, one_hot(size, far_skel[slot, pl.ds(leaf, 1), :])).astype(BF)
        skel_columns[(slot + 1) * leaves + leaf] = jnp.transpose(picked)

    def columns_of(slot, first, count):
        def step(leaf, _):
            passed_columns(slot, leaf)
            return 0

        lax.fori_loop(first, first + count, step, 0, unroll=4)

    def self_blocks(first, count):
        def step(i, _):
            at = first + 4 * i
            for u in range(4):
                tiles[u] = tile(leaf_columns[at + u], leaf_rows[at + u], scale)
            for u in range(4):
                self_part[at + u] = dot(signs[at + u], tiles[u])
            return 0

        lax.fori_loop(0, count // 4, step, 0)

    def pass_on(*which):
        for k in which:
            own_copy(k).wait_recv()
            passed_copy(k).start()

    def pack_queues():
        own_copy(6).wait_recv()
        row = jnp.concatenate([lists[0], lists[1]], axis=1)
        lane = lax.broadcasted_iota(I32, (1, 256), 1)
        mine = lane < 128
        spot = lane & 127
        before = jnp.where(
            lax.broadcasted_iota(I32, (256, 256), 0) < lax.broadcasted_iota(I32, (256, 256), 1), 1.0, 0.0
        ).astype(BF)
        eight = lax.broadcasted_iota(I32, (8, 256), 0)
        for first, second, count, packed in (
            (row[0:1], row[1:2], row[4:5], near_packed),
            (row[2:3], row[3:4], far_pairs.shape[1], far_packed),
        ):
            holder = second >> 4
            slot = ((holder - place) * (1 + 2 * odd)) & 3
            wanted = jnp.where(mine, jnp.where(slot == 3, 0, 1), jnp.where(holder == place, 1, 0))
            keep = jnp.where(spot < count, wanted, 0)
            inner = jnp.where(mine, first, second & 15)
            outer = jnp.where(mine, slot * 16 + (second & 15), 16 + first) - 48
            keep_f = jnp.where(keep == 1, 1.0, 0.0)
            total = jnp.sum(keep_f, axis=1, keepdims=True)
            rank = dot(jnp.broadcast_to(keep_f, (8, 256)).astype(BF), before)[0:1]
            rank = jnp.where(keep == 1, rank, -1.0)
            chosen = jnp.where(
                lax.broadcasted_iota(I32, (QUEUE, 256), 0).astype(F32) == rank, 1.0, 0.0
            ).astype(BF)
            codes = jnp.where(eight == 0, inner, outer).astype(F32).astype(BF)
            taken = dot(codes, chosen, 1, 1)
            taken = jnp.where(eight == 0, taken, taken + 48.0)
            packed[...] = jnp.where(eight == 2, total, taken).astype(I32)
        pltpu.make_async_copy(near_packed, near_queue, queue_sem.at[0]).start()
        pltpu.make_async_copy(far_packed, far_queue, queue_sem.at[1]).start()

    def state_copy(t):
        side = (tree >> t) & 1
        return pltpu.make_async_remote_copy(
            src_ref=states.at[t, side],
            dst_ref=states.at[t, side],
            send_sem=state_send.at[t],
            recv_sem=state_recv.at[t],
            device_id={"leaf": partners[t]},
            device_id_type=MESH,
        )

    def put_state(t, state_coords, state_weights):
        side = (tree >> t) & 1
        states[t, side, 0:features] = state_coords.astype(BF)
        states[t, side, features:] = state_weights.astype(BF)
        state_copy(t).start()

    def far_term(t):
        side = (tree >> t) & 1
        mine = states[t, side, 0:features]
        other = states[t, 1 - side]
        other_coords = other[0:features]
        block = tile(
            jnp.transpose(column_form(other_coords, norm_parts(other_coords))),
            row_form(mine, norm_parts(mine)),
            scale,
        )
        far_own[t] = dot(other[features:], block)

    lax.fori_loop(0, leaves, own_columns, 0, unroll=4)
    signs[3 * leaves] = jnp.zeros_like(signs[3 * leaves])
    weights[3 * leaves] = jnp.zeros_like(weights[3 * leaves])
    leaf_columns[3 * leaves] = jnp.zeros_like(leaf_columns[3 * leaves])
    skel_columns[3 * leaves] = jnp.zeros_like(skel_columns[3 * leaves])

    for k in range(1, 4):
        node_copy(k).wait_recv()
    group = jnp.concatenate([nodes[s] for s in range(4)], axis=1)
    put_state(
        0,
        dot(group[0:features], one_hot(group.shape[1], subtree_skel[...])),
        dot(group[features:], subtree_basis[0], 1, 1),
    )

    half = leaves // 2

    def part_a():
        pass_on(5, 0, 1)
        self_blocks(0, 4)

    def part_b():
        pass_on(2, 3)
        columns_of(0, 0, half)

    def part_c():
        pack_queues()
        self_blocks(4, 4)

    def part_d():
        pass_on(4, 7)
        columns_of(0, half, half)

    def part_e():
        self_blocks(8, 8)
        passed_copy(5).wait_recv()

    def part_f():
        passed_copy(0).wait_recv()
        columns_of(1, 0, quarter)

    gaps = [part_a, part_b, part_c, part_d, part_e, part_f]
    for t in range(levels):
        if t < len(gaps):
            gaps[t]()
        state_copy(t).wait_recv()
        if t + 1 < levels:
            both = jnp.concatenate([states[t, 0], states[t, 1]], axis=1)
            put_state(
                t + 1,
                dot(both[0:features], one_hot(both.shape[1], upper_skel[0, t : t + 1, :])),
                dot(both[features:], upper_basis[0, t], 1, 1),
            )
        far_term(t)
    for gap in gaps[levels:]:
        gap()
    for k in range(1, 4):
        passed_copy(k).wait_recv()
        columns_of(1, k * quarter, quarter)
    passed_copy(4).wait_recv()
    passed_copy(7).wait_recv()

    for k in range(8):
        own_copy(k).wait_send()
        if k != 6:
            passed_copy(k).wait_send()
    for k in range(1, 4):
        node_copy(k).wait_send()
    for t in range(levels):
        state_copy(t).wait_send()
    pltpu.make_async_copy(near_packed, near_queue, queue_sem.at[0]).wait()
    pltpu.make_async_copy(far_packed, far_queue, queue_sem.at[1]).wait()


def pair_kernel(
    leaves,
    features,
    near_queue,
    far_queue,
    leaf_columns,
    leaf_rows,
    skel_columns,
    skel_rows,
    signs,
    weights,
    near_own,
    far_own,
    near_out,
    far_out,
    near_sum,
    far_sum,
    near_tiles,
    far_tiles,
):
    scale = math.log2(math.e) / features
    near_sum[...] = jnp.zeros_like(near_sum)
    far_sum[...] = jnp.zeros_like(far_sum)

    def run(queue, group, columns, rows, vectors, tiles, total, rounded):
        groups = (queue[2, 0] + 2 * group - 1) // (2 * group)

        def first_tiles():
            for u in range(group):
                tiles[0, u] = tile(columns[queue[1, u]], rows[queue[0, u]], scale)

        def half(make, to, use, source):
            found = []
            for u in range(group):
                inner = queue[0, use * group + u]
                outer = queue[1, use * group + u]
                block = tiles[source, u]
                to_inner = dot(vectors[outer], block)
                to_outer = dot(vectors[inner], block, 1, 1)
                if rounded:
                    to_inner = to_inner.astype(BF).astype(F32)
                    to_outer = to_outer.astype(BF).astype(F32)
                found.append((inner, outer, to_inner, to_outer))
                tiles[to, u] = tile(
                    columns[queue[1, make * group + u]], rows[queue[0, make * group + u]], scale
                )
            for inner, outer, to_inner, to_outer in found:
                total[inner] += to_inner
                total[outer] += to_outer

        def step(i, _):
            half(2 * i + 1, 1, 2 * i, 0)
            half(jnp.minimum(2 * i + 2, QUEUE // group - 1), 0, 2 * i + 1, 1)
            return 0

        first_tiles()
        lax.fori_loop(0, groups, step, 0)

    run(far_queue, FAR_GROUP, skel_columns, skel_rows, weights, far_tiles, far_sum, True)
    run(near_queue, NEAR_GROUP, leaf_columns, leaf_rows, signs, near_tiles, near_sum, False)
    near_own[...] = near_sum[0:leaves]
    far_own[...] = far_sum[0:leaves]
    near_out[...] = near_sum[leaves : 3 * leaves].astype(BF)
    far_out[...] = far_sum[leaves : 3 * leaves].astype(BF)


def downward_kernel(
    levels,
    near_own,
    far_leaf,
    near_out,
    far_out,
    self_part,
    far_own,
    leaf_basis,
    device_basis,
    subtree_basis,
    upper_basis,
    product,
    near_in,
    far_in,
    spread,
    send_sem,
    recv_sem,
):
    leaves = near_own.shape[0]
    place = lax.axis_index("sub")
    tree = lax.axis_index("leaf")
    odd = tree & 1
    ahead = (place + 1 + 2 * odd) & 3
    across = (place + 2) & 3
    barrier = pltpu.get_barrier_semaphore()
    for k in range(1, 4):
        pl.semaphore_signal(barrier, inc=1, device_id={"sub": (place + k) & 3}, device_id_type=MESH)
    pl.semaphore_wait(barrier, 3)

    def copy(k):
        slot, far = k // 2, k % 2
        source, target = (far_out, far_in) if far else (near_out, near_in)
        return pltpu.make_async_remote_copy(
            src_ref=source.at[pl.ds(slot * leaves, leaves)],
            dst_ref=target.at[slot],
            send_sem=send_sem.at[k],
            recv_sem=recv_sem.at[k],
            device_id={"sub": across if slot else ahead},
            device_id_type=MESH,
        )

    for k in (3, 1, 2, 0):
        copy(k).start()

    potential = far_own[levels - 1]
    for t in range(levels - 2, -1, -1):
        side = (tree >> t) & 1
        lane = pl.ds(pl.multiple_of(side * 128, 128), 128)
        potential = far_own[t] + dot(potential.astype(BF), upper_basis[0, t, :, lane])
    lane = pl.ds(pl.multiple_of(place * 128, 128), 128)
    potential = dot(potential.astype(BF), subtree_basis[0, :, lane])
    spread[...] = dot(potential.astype(BF), device_basis[0]).astype(BF)

    def tree_step(leaf, _):
        lane = pl.ds(pl.multiple_of(leaf * 128, 128), 128)
        product[leaf] = near_own[leaf] + self_part[leaf] + dot(spread[:, lane], leaf_basis[leaf])
        return 0

    lax.fori_loop(0, leaves, tree_step, 0, unroll=4)
    for k in range(4):
        copy(k).wait_recv()

    def last_step(leaf, _):
        far = far_leaf[leaf] + far_in[0, leaf].astype(F32) + far_in[1, leaf].astype(F32)
        high = far.astype(BF)
        low = (far - high.astype(F32)).astype(BF)
        both = dot(jnp.concatenate([high, low], axis=0), leaf_basis[leaf])
        near = near_in[0, leaf].astype(F32) + near_in[1, leaf].astype(F32)
        product[leaf] = product[leaf] + near + both[0:16] + both[16:32]
        return 0

    lax.fori_loop(0, leaves, last_step, 0, unroll=4)
    for k in range(4):
        copy(k).wait_send()


def on_device(
    points,
    probe_bits,
    leaf_skel,
    leaf_basis,
    device_skel,
    device_basis,
    subtree_skel,
    subtree_basis,
    upper_skel,
    upper_basis,
    near_pairs,
    near_count,
    far_pairs,
):
    leaves, features, size = points.shape
    probes = probe_bits.shape[1]
    skeleton = leaf_skel.shape[1]
    levels = upper_basis.shape[1] + 1
    known = 3 * leaves + 1
    limit = 40 << 20
    (
        leaf_columns,
        leaf_rows,
        skel_columns,
        skel_rows,
        signs,
        weights,
        self_part,
        far_own,
        near_queue,
        far_queue,
    ) = pl.pallas_call(
        functools.partial(upward_kernel, levels),
        out_shape=(
            pltpu.VMEM((known, size, 128), BF),
            pltpu.VMEM((leaves, 128, size), BF),
            pltpu.VMEM((known, skeleton, 128), BF),
            pltpu.VMEM((leaves, 128, skeleton), BF),
            pltpu.VMEM((known, probes, size), BF),
            pltpu.VMEM((known, probes, skeleton), BF),
            pltpu.VMEM((leaves, probes, size), F32),
            pltpu.VMEM((levels, probes, skeleton), F32),
            pltpu.SMEM((8, QUEUE), I32),
            pltpu.SMEM((8, QUEUE), I32),
        ),
        in_specs=[VM] * 11 + [SM, VM],
        out_specs=(VM,) * 8 + (SM, SM),
        scratch_shapes=[
            pltpu.VMEM((2, leaves, features, size), BF),
            pltpu.VMEM((2, leaves, skeleton), I32),
            pltpu.VMEM((features + probes, leaves * skeleton), BF),
            pltpu.VMEM((4, features + probes, skeleton), BF),
            pltpu.VMEM((levels, 2, features + probes, skeleton), BF),
            pltpu.VMEM((2, 8, 128), I32),
            pltpu.VMEM((4, size, size), BF),
            pltpu.VMEM((8, QUEUE), I32),
            pltpu.VMEM((8, QUEUE), I32),
            pltpu.SemaphoreType.DMA((16,)),
            pltpu.SemaphoreType.DMA((8,)),
            pltpu.SemaphoreType.DMA((8,)),
            pltpu.SemaphoreType.DMA((3,)),
            pltpu.SemaphoreType.DMA((3,)),
            pltpu.SemaphoreType.DMA((levels,)),
            pltpu.SemaphoreType.DMA((levels,)),
            pltpu.SemaphoreType.DMA((2,)),
        ],
        compiler_params=pltpu.CompilerParams(
            collective_id=1, has_side_effects=True, vmem_limit_bytes=limit
        ),
        name="upward",
    )(
        points,
        probe_bits,
        leaf_skel,
        leaf_basis,
        device_skel,
        device_basis,
        subtree_skel,
        subtree_basis,
        upper_skel,
        upper_basis,
        near_pairs,
        near_count,
        far_pairs,
    )
    near_own, far_leaf, near_out, far_out = pl.pallas_call(
        functools.partial(pair_kernel, leaves, features),
        out_shape=(
            pltpu.VMEM((leaves, probes, size), F32),
            pltpu.VMEM((leaves, probes, skeleton), F32),
            pltpu.VMEM((2 * leaves, probes, size), BF),
            pltpu.VMEM((2 * leaves, probes, skeleton), BF),
        ),
        in_specs=[SM, SM] + [VM] * 6,
        out_specs=(VM,) * 4,
        scratch_shapes=[
            pltpu.VMEM((known, probes, size), F32),
            pltpu.VMEM((known, probes, skeleton), F32),
            pltpu.VMEM((2, NEAR_GROUP, size, size), BF),
            pltpu.VMEM((2, FAR_GROUP, skeleton, skeleton), BF),
        ],
        compiler_params=pltpu.CompilerParams(vmem_limit_bytes=limit),
        name="pairs",
    )(near_queue, far_queue, leaf_columns, leaf_rows, skel_columns, skel_rows, signs, weights)
    return pl.pallas_call(
        functools.partial(downward_kernel, levels),
        out_shape=jax.ShapeDtypeStruct((leaves, probes, size), F32),
        in_specs=[VM] * 10,
        out_specs=VM,
        scratch_shapes=[
            pltpu.VMEM((2, leaves, probes, size), BF),
            pltpu.VMEM((2, leaves, probes, skeleton), BF),
            pltpu.VMEM((probes, leaves * skeleton), BF),
            pltpu.SemaphoreType.DMA((4,)),
            pltpu.SemaphoreType.DMA((4,)),
        ],
        compiler_params=pltpu.CompilerParams(
            collective_id=2, has_side_effects=True, vmem_limit_bytes=limit
        ),
        name="downward",
    )(
        near_own,
        far_leaf,
        near_out,
        far_out,
        self_part,
        far_own,
        leaf_basis,
        device_basis,
        subtree_basis,
        upper_basis,
    )


def solution(mesh):
    return jax.shard_map(
        on_device,
        mesh=mesh,
        in_specs=(
            P(("leaf", "sub"), None, None),
            P(("leaf", "sub"), None, None),
            P(("leaf", "sub"), None),
            P(("leaf", "sub"), None, None),
            P(("leaf", "sub"), None),
            P(("leaf", "sub"), None, None),
            P("leaf", None),
            P("leaf", None, None),
            P("leaf", None, None),
            P("leaf", None, None, None),
            P(("leaf", "sub"), None, None),
            P(("leaf", "sub")),
            P(("leaf", "sub"), None, None),
        ),
        out_specs=P(("leaf", "sub"), None, None),
        check_vma=False,
    )
```

time: 413 us -> 83.8 us (0.20)
  the two profiles are of different devices: /device:TPU:8 before, /device:TPU:56 now
where the time goes in v1:
time: 83.8 us; the launch traced here: 83.3 us
  Pallas kernels  71.4 us (85%)
  local copies, waits for them, and re-layouts  11.1 us (13%)
    pallas_call x1, Pallas kernels, on_device(): pl.pallas_call(functools.partial(upward_kernel, levels), out_shape=(pltpu...  49.6 us
    pallas_call x1, Pallas kernels, on_device(): pl.pallas_call(functools.partial(downward_kernel, levels), out_shape=jax....  14.2 us
    unnamed x30, local copies, waits for them, and re-layouts  11.1 us
    pallas_call x1, Pallas kernels, on_device(): pl.pallas_call(functools.partial(pair_kernel, leaves, features), out_shap...  7.64 us

profile of v1, /device:TPU:56, one launch (start us, length us, event | category | flops | bytes accessed | tf_op | source)
XLA Modules:
  0.0 83.3 jit_solution(1953051809918235231)
XLA Ops:
  0.7 0.7 copy.14.upper_skel
  1.3 0.8 copy.15.near_pairs
  2.1 0.8 copy.16.far_pairs
  2.9 0.0 copy-start
  2.9 1.2 %copy-done = bf16[16,128,256]{2,1,0:T(8,128)(2,1)S(1)} copy-done((bf16[16,128,256]{2,1,0:T(8,128)(2,1)S(1)}, bf16[16,128,256]{2,1,0:T(8,128)(2,1)}, u32[]{:S(2)}) %copy-start) | copy-done | bytes 1048600
  4.1 0.0 copy-start.2
  4.1 1.0 %copy-done.2 = bf16[1,128,2048]{2,1,0:T(8,128)(2,1)S(1)} copy-done((bf16[1,128,2048]{2,1,0:T(8,128)(2,1)S(1)}, bf16[1,128,2048]{2,1,0:T(8,128)(2,1)}, u32[]{:S(2)}) %copy-start.2) | copy-done | bytes 524312
  5.2 0.0 copy-start.4
  5.2 1.0 %copy-done.4 = bf16[1,6,128,256]{3,2,1,0:T(8,128)(2,1)S(1)} copy-done((bf16[1,6,128,256]{3,2,1,0:T(8,128)(2,1)S(1)}, bf16[1,6,128,256]{3,2,1,0:T(8,128)(2,1)}, u32[]{:S(2)}) %copy-start.4) | copy-done | bytes 393240
  6.2 0.0 copy-start.6
  6.2 1.0 %copy-done.6 = bf16[16,64,256]{2,1,0:T(8,128)(2,1)S(1)} copy-done((bf16[16,64,256]{2,1,0:T(8,128)(2,1)S(1)}, bf16[16,64,256]{2,1,0:T(8,128)(2,1)}, u32[]{:S(2)}) %copy-start.6) | copy-done | bytes 524312
  7.2 0.0 copy-start.7
  7.2 0.9 %copy-done.7 = bf16[1,128,512]{2,1,0:T(8,128)(2,1)S(1)} copy-done((bf16[1,128,512]{2,1,0:T(8,128)(2,1)S(1)}, bf16[1,128,512]{2,1,0:T(8,128)(2,1)}, u32[]{:S(2)}) %copy-start.7) | copy-done | bytes 131096
  8.1 0.0 copy-start.9
  8.1 0.9 %copy-done.9 = s32[16,16,256]{2,1,0:T(8,128)S(1)} copy-done((s32[16,16,256]{2,1,0:T(8,128)S(1)}, s32[16,16,256]{2,1,0:T(8,128)}, u32[]{:S(2)}) %copy-start.9) | copy-done | bytes 262168
  9.1 0.7 copy-done.10
  9.7 0.0 copy-start.11
  9.7 0.7 copy-done.11
  10.4 0.0 copy-start.12
  10.4 0.7 copy-done.12
  11.1 49.6 %upward.1 = (bf16[49,256,128]{2,1,0:T(8,128)(2,1)S(1)}, bf16[16,128,256]{2,1,0:T(8,128)(2,1)S(1)}, bf16[49,128,128]{2,1,0:T(8,128)(2,1)S(1)}, bf16[16,128,128]{2...) custom-call(bf16[16,64,256]{2,1,0:T(8,128)(2,1)S(1)} %copy-done.6, ...), custom_call_target="tpu_custom_call" | custom-call | tf_op jit(solution)/shard_map/upward/pallas_call | solution.py:566
  60.7 0.0 copy-start.1
  60.7 0.0 copy-start.3
  60.7 0.0 copy-start.5
  60.7 0.0 copy-start.8
  60.7 7.6 %pairs.1 = (f32[16,16,256]{2,1,0:T(8,128)S(1)}, f32[16,16,128]{2,1,0:T(8,128)S(1)}, bf16[32,16,256]{2,1,0:T(8,128)(2,1)S(1)}, bf16[32,16,128]{2,1,0:T(8,128)(2,1)S(1)}) custom-call(s32[8,256]{1,0:T(8,128)S(4)} %get-tuple-element.19.near_queue, s32[8,256]{1,0:T(8,128)S(4)} %get-tuple-element.20.far_queue, ...), custom_call_target="tpu_custom_call" | custom-call | tf_op jit(solution)/shard_map/pairs/pallas_call | solution.py:620
  68.4 0.0 copy-done.1
  68.4 0.0 copy-done.3
  68.4 0.0 copy-done.5
  68.4 0.0 copy-done.8
  68.4 14.2 %downward.1 = f32[16,16,256]{2,1,0:T(8,128)S(1)} custom-call(f32[16,16,256]{2,1,0:T(8,128)S(1)} %get-tuple-element.27.near_own, f32[16,16,128]{2,1,0:T(8,128)S(1)} %get-tuple-element.28.far_leaf, bf16[32,16,256]{2,1,0:T(8,128)(2,1)S(1)} %get-tuple-element.29.near_out, bf16[32,16,128]{2,1,0:T(8,128)(2,1)S(1)} %get-tuple-element.30.far_out, ...), custom_call_target="tpu_custom_call" | custom-call | tf_op jit(solution)/shard_map/downward/pallas_call | solution.py:639
  82.6 0.7 copy.19
  (1 shorter events, 0.0 us)
Async XLA Ops:
  2.9 1.2 %copy-start = (bf16[16,128,256]{2,1,0:T(8,128)(2,1)S(1)}, bf16[16,128,256]{2,1,0:T(8,128)(2,1)}, u32[]{:S(2)}) copy-start(bf16[16,128,256]{2,1,0:T(8,128)(2,1)} %leaf_basis.3) | copy-start | bytes 3145732
  4.1 1.0 %copy-start.2 = (bf16[1,128,2048]{2,1,0:T(8,128)(2,1)S(1)}, bf16[1,128,2048]{2,1,0:T(8,128)(2,1)}, u32[]{:S(2)}) copy-start(bf16[1,128,2048]{2,1,0:T(8,128)(2,1)} %device_basis.3) | copy-start | bytes 1572868
  5.2 1.0 %copy-start.4 = (bf16[1,6,128,256]{3,2,1,0:T(8,128)(2,1)S(1)}, bf16[1,6,128,256]{3,2,1,0:T(8,128)(2,1)}, u32[]{:S(2)}) copy-start(bf16[1,6,128,256]{3,2,1,0:T(8,128)(2,1)} %upper_basis.3) | copy-start | bytes 1179652
  6.2 1.0 %copy-start.6 = (bf16[16,64,256]{2,1,0:T(8,128)(2,1)S(1)}, bf16[16,64,256]{2,1,0:T(8,128)(2,1)}, u32[]{:S(2)}) copy-start(bf16[16,64,256]{2,1,0:T(8,128)(2,1)} %points.1) | copy-start | bytes 1572868
  7.2 0.9 %copy-start.7 = (bf16[1,128,512]{2,1,0:T(8,128)(2,1)S(1)}, bf16[1,128,512]{2,1,0:T(8,128)(2,1)}, u32[]{:S(2)}) copy-start(bf16[1,128,512]{2,1,0:T(8,128)(2,1)} %subtree_basis.3) | copy-start | bytes 393220
  8.1 0.9 %copy-start.9 = (s32[16,16,256]{2,1,0:T(8,128)S(1)}, s32[16,16,256]{2,1,0:T(8,128)}, u32[]{:S(2)}) copy-start(s32[16,16,256]{2,1,0:T(8,128)} %bits.1) | copy-start | bytes 786436
  9.0 0.7 copy-start.10
  9.7 0.7 copy-start.11
  10.4 0.7 copy-start.12
  60.7 7.7 %copy-start.1 = (bf16[16,128,256]{2,1,0:T(8,128)(2,1)S(1)}, bf16[16,128,256]{2,1,0:T(8,128)(2,1)}, u32[]{:S(2)}) copy-start(bf16[16,128,256]{2,1,0:T(8,128)(2,1)} %leaf_basis.3) | copy-start | bytes 3145732
  60.7 7.7 %copy-start.3 = (bf16[1,128,2048]{2,1,0:T(8,128)(2,1)S(1)}, bf16[1,128,2048]{2,1,0:T(8,128)(2,1)}, u32[]{:S(2)}) copy-start(bf16[1,128,2048]{2,1,0:T(8,128)(2,1)} %device_basis.3) | copy-start | bytes 1572868
  60.7 7.7 %copy-start.5 = (bf16[1,6,128,256]{3,2,1,0:T(8,128)(2,1)S(1)}, bf16[1,6,128,256]{3,2,1,0:T(8,128)(2,1)}, u32[]{:S(2)}) copy-start(bf16[1,6,128,256]{3,2,1,0:T(8,128)(2,1)} %upper_basis.3) | copy-start | bytes 1179652
  60.7 7.7 %copy-start.8 = (bf16[1,128,512]{2,1,0:T(8,128)(2,1)S(1)}, bf16[1,128,512]{2,1,0:T(8,128)(2,1)}, u32[]{:S(2)}) copy-start(bf16[1,128,512]{2,1,0:T(8,128)(2,1)} %subtree_basis.3) | copy-start | bytes 393220

commit v2 on v1

v2 whole, which is shorter than its diff:
```python
import functools
import math

import jax
import jax.numpy as jnp
from jax import lax
from jax.experimental import pallas as pl
from jax.experimental.pallas import tpu as pltpu
from jax.sharding import PartitionSpec as P

F32 = jnp.float32
BF = jnp.bfloat16
I32 = jnp.int32
MESH = pl.DeviceIdType.MESH
VM = pl.BlockSpec(memory_space=pltpu.VMEM)
SM = pl.BlockSpec(memory_space=pltpu.SMEM)
HB = pl.BlockSpec(memory_space=pltpu.HBM)
NEAR_GROUPS = (6, 4)
FAR_GROUPS = (12, 8)
QUEUE = 240


def dot(a, b, ca=1, cb=0):
    return lax.dot_general(a, b, (((ca,), (cb,)), ((), ())), preferred_element_type=F32)


def one_hot(rows, row):
    spot = lax.broadcasted_iota(I32, (rows, row.shape[1]), 0) == row
    return jnp.where(spot, 1.0, 0.0).astype(BF)


def norm_parts(coords):
    wide = coords.astype(F32)
    norm = jnp.sum(wide * wide, axis=0, keepdims=True)
    high = norm.astype(BF).astype(F32)
    rest = norm - high
    middle = rest.astype(BF).astype(F32)
    return -high, -middle, middle - rest


def row_form(coords, parts):
    high, middle, low = parts
    at = lax.broadcasted_iota(I32, (16, coords.shape[1]), 0)
    tail = jnp.where(
        at < 3, 1.0, jnp.where(at == 3, high, jnp.where(at == 4, middle, jnp.where(at == 5, low, 0.0)))
    )
    return jnp.concatenate(
        [coords, tail.astype(BF), jnp.zeros((48, coords.shape[1]), BF)], axis=0
    )


def column_form(coords, parts):
    high, middle, low = parts
    at = lax.broadcasted_iota(I32, (16, coords.shape[1]), 0)
    tail = jnp.where(
        at == 0, high, jnp.where(at == 1, middle, jnp.where(at == 2, low, jnp.where(at < 6, 1.0, 0.0)))
    )
    return jnp.concatenate(
        [coords + coords, tail.astype(BF), jnp.zeros((48, coords.shape[1]), BF)], axis=0
    )


def tile(columns, rows, scale):
    return jnp.exp2(dot(columns, rows) * scale).astype(BF)


def plan(levels):
    rounds, low = [], 0
    while low < levels:
        left = levels - low
        count = left if left <= 3 else 2
        rounds.append((low, count))
        low += count
    return rounds


def widths(levels):
    return [1 << (low + count - t) for low, count in plan(levels) for t in range(low, low + count)]


def upward_kernel(
    levels,
    points_in,
    bits_in,
    leaf_skel_in,
    leaf_basis_in,
    device_skel_in,
    device_basis_in,
    subtree_skel_in,
    subtree_basis_in,
    upper_skel_in,
    upper_basis_in,
    near_in,
    near_count,
    far_in,
    leaf_columns,
    leaf_rows,
    skel_columns,
    skel_rows,
    signs,
    weights,
    base,
    leaf_basis,
    queues,
    points,
    bits,
    leaf_skel,
    device_skel,
    device_basis,
    subtree_skel,
    subtree_basis,
    near_pairs,
    far_pairs,
    far_points,
    far_skel,
    joined,
    nodes,
    lists,
    tiles,
    packed,
    far_own,
    spread,
    states,
    bases,
    skels,
    hots,
    load_sem,
    send_sem,
    recv_sem,
    pass_sem,
    node_send,
    node_recv,
    state_send,
    state_recv,
    basis_send,
    basis_recv,
    queue_sem,
):
    leaves, features, size = points.shape
    scale = math.log2(math.e) / features
    place = lax.axis_index("sub")
    tree = lax.axis_index("leaf")
    odd = tree & 1
    behind = (place + 3 - 2 * odd) & 3
    rounds = plan(levels)
    wide = widths(levels)
    peers = [
        (low, m, tree ^ (m << low)) for low, count in rounds for m in range(1, 1 << count)
    ]

    barrier = pltpu.get_barrier_semaphore()
    for k in range(1, 4):
        pl.semaphore_signal(barrier, inc=1, device_id={"sub": (place + k) & 3}, device_id_type=MESH)
    for _, _, peer in peers:
        pl.semaphore_signal(barrier, inc=1, device_id={"leaf": peer}, device_id_type=MESH)

    loads = [
        (bits_in, bits),
        (near_in, near_pairs),
        (far_in, far_pairs),
        (points_in, points),
        (leaf_skel_in, leaf_skel),
        (leaf_basis_in, leaf_basis),
        (device_skel_in, device_skel),
        (device_basis_in, device_basis),
        (subtree_skel_in, subtree_skel),
        (subtree_basis_in, subtree_basis),
    ]
    for t in range(levels - 1):
        held = (tree >> (t + 1)) & (wide[t] // 2 - 1)
        loads.append((upper_basis_in.at[0, t], bases[t].at[held]))
        loads.append((upper_skel_in.at[t], skels[t].at[held]))

    def load(k):
        return pltpu.make_async_copy(loads[k][0], loads[k][1], load_sem.at[k])

    for k in range(len(loads)):
        load(k).start()

    load(0).wait()

    def make_signs(leaf, _):
        signs[leaf] = (2 * bits[leaf] - 1).astype(F32).astype(BF)
        return 0

    lax.fori_loop(0, leaves, make_signs, 0, unroll=4)
    load(1).wait()
    load(2).wait()
    lists[0] = jnp.zeros((8, 128), I32)
    lists[0, 0:2, 0 : near_pairs.shape[2]] = near_pairs[0]
    lists[0, 2:4, 0 : far_pairs.shape[2]] = far_pairs[0]
    lists[0, 4:5, :] = jnp.full((1, 128), near_count[0], I32)

    for k in range(3, len(loads)):
        load(k).wait()

    def leaf_step(leaf, _):
        coords = points[leaf]
        rows = row_form(coords, norm_parts(coords))
        leaf_rows[leaf] = rows
        picked = dot(rows, one_hot(size, leaf_skel[pl.ds(leaf, 1), :])).astype(BF)
        skel_rows[leaf] = picked
        lane = pl.ds(pl.multiple_of(leaf * 128, 128), 128)
        joined[0:features, lane] = picked[0:features]
        weight = dot(signs[leaf], leaf_basis[leaf], 1, 1).astype(BF)
        weights[leaf] = weight
        joined[features:, lane] = weight
        return 0

    lax.fori_loop(0, leaves, leaf_step, 0, unroll=4)
    pl.semaphore_wait(barrier, 3 + len(peers))

    quarter = leaves // 4

    def remote(source, target, sent, received, device):
        return pltpu.make_async_remote_copy(
            src_ref=source,
            dst_ref=target,
            send_sem=sent,
            recv_sem=received,
            device_id=device,
            device_id_type=MESH,
        )

    def own_copy(k):
        if k < 4:
            part = pl.ds(k * quarter, quarter)
            pair = (points_in.at[part], far_points.at[0, part])
        elif k == 4:
            pair = (signs.at[pl.ds(0, leaves)], signs.at[pl.ds(leaves, leaves)])
        elif k == 5:
            pair = (leaf_skel_in, far_skel.at[0])
        elif k == 6:
            pair = (lists.at[0], lists.at[1])
        else:
            pair = (weights.at[pl.ds(0, leaves)], weights.at[pl.ds(leaves, leaves)])
        return remote(*pair, send_sem.at[k], recv_sem.at[k], {"sub": behind})

    def passed_copy(k):
        if k < 4:
            part = pl.ds(k * quarter, quarter)
            pair = (far_points.at[0, part], far_points.at[1, part])
        elif k == 4:
            pair = (signs.at[pl.ds(leaves, leaves)], signs.at[pl.ds(2 * leaves, leaves)])
        elif k == 5:
            pair = (far_skel.at[0], far_skel.at[1])
        elif k == 6:
            pair = (lists.at[1], lists.at[2])
        else:
            pair = (weights.at[pl.ds(leaves, leaves)], weights.at[pl.ds(2 * leaves, leaves)])
        return remote(*pair, send_sem.at[8 + k], pass_sem.at[k], {"sub": behind})

    for k in (5, 6, 0, 1, 2, 3, 4, 7):
        own_copy(k).start()

    nodes[place, 0:features] = dot(
        joined[0:features], one_hot(joined.shape[1], device_skel[...])
    ).astype(BF)
    nodes[place, features:] = dot(joined[features:], device_basis[0], 1, 1).astype(BF)

    def node_copy(k):
        return remote(
            nodes.at[place],
            nodes.at[place],
            node_send.at[k - 1],
            node_recv.at[k - 1],
            {"sub": (place + k) & 3},
        )

    for k in range(1, 4):
        node_copy(k).start()

    basis_copies = []
    for t in range(levels - 1):
        held = (tree >> (t + 1)) & (wide[t] // 2 - 1)
        for q in range(1, wide[t] // 2):
            device = {"leaf": tree ^ (q << (t + 1))}
            for source, target in (
                (upper_basis_in.at[0, t], bases[t].at[held]),
                (upper_skel_in.at[t], skels[t].at[held]),
            ):
                n = len(basis_copies)
                basis_copies.append(
                    remote(source, target, basis_send.at[n], basis_recv.at[n], device)
                )
    for copy in basis_copies:
        copy.start()


    def own_columns(leaf, _):
        coords = points[leaf]
        leaf_columns[leaf] = jnp.transpose(column_form(coords, norm_parts(coords)))
        coords = skel_rows[leaf, 0:features]
        skel_columns[leaf] = jnp.transpose(column_form(coords, norm_parts(coords)))
        return 0

    def columns_of(slot, first, count):
        def step(leaf, _):
            coords = far_points[slot, leaf]
            columns = column_form(coords, norm_parts(coords))
            leaf_columns[(slot + 1) * leaves + leaf] = jnp.transpose(columns)
            picked = dot(columns, one_hot(size, far_skel[slot, pl.ds(leaf, 1), :])).astype(BF)
            skel_columns[(slot + 1) * leaves + leaf] = jnp.transpose(picked)
            return 0

        lax.fori_loop(first, first + count, step, 0, unroll=4)

    def self_blocks(first, count):
        def step(i, _):
            at = first + 4 * i
            for u in range(4):
                tiles[u] = tile(leaf_columns[at + u], leaf_rows[at + u], scale)
            for u in range(4):
                base[at + u] = dot(signs[at + u], tiles[u])
            return 0

        lax.fori_loop(0, count // 4, step, 0)

    def pass_on(*which):
        for k in which:
            own_copy(k).wait_recv()
            passed_copy(k).start()

    def pack_queues():
        passed_copy(6).wait_recv()
        row = jnp.concatenate([lists[0], lists[1], lists[2]], axis=1)
        lane = lax.broadcasted_iota(I32, (1, 384), 1)
        origin = lane >> 7
        spot = lane & 127
        before = jnp.where(
            lax.broadcasted_iota(I32, (384, 384), 0) < lax.broadcasted_iota(I32, (384, 384), 1), 1.0, 0.0
        ).astype(BF)
        eight = lax.broadcasted_iota(I32, (8, 384), 0)
        eight_out = lax.broadcasted_iota(I32, (8, QUEUE), 0)
        for which, first, second, count in (
            (0, row[0:1], row[1:2], row[4:5]),
            (2, row[2:3], row[3:4], far_pairs.shape[2]),
        ):
            holder = second >> 4
            slot = ((holder - place) * (1 + 2 * odd)) & 3
            inner = jnp.where(origin == 0, first, second & 15)
            outer = jnp.where(origin == 0, slot, origin) * 16
            outer = outer + jnp.where(origin == 0, second & 15, first) - 48
            here = jnp.where(slot == 0, 1, 0)
            both_sides = jnp.where(origin == 0, jnp.where(slot < 2, 1, 0), jnp.where(origin == 1, here, 0))
            one_side = jnp.where(
                origin == 0, jnp.where(slot == 2, 1, 0), jnp.where(origin == 2, here, 0)
            )
            codes = jnp.where(eight == 0, inner, outer).astype(F32).astype(BF)
            for side, wanted in enumerate((both_sides, one_side)):
                keep = jnp.where(spot < count, wanted, 0)
                keep_f = jnp.where(keep == 1, 1.0, 0.0)
                total = jnp.sum(keep_f, axis=1, keepdims=True)
                rank = dot(jnp.broadcast_to(keep_f, (8, 384)).astype(BF), before)[0:1]
                rank = jnp.where(keep == 1, rank, -1.0)
                chosen = jnp.where(
                    lax.broadcasted_iota(I32, (QUEUE, 384), 0).astype(F32) == rank, 1.0, 0.0
                ).astype(BF)
                taken = dot(codes, chosen, 1, 1)
                taken = jnp.where(eight_out == 0, taken, taken + 48.0)
                packed[which + side] = jnp.where(eight_out == 2, total, taken).astype(I32)
        pltpu.make_async_copy(packed, queues, queue_sem.at[0]).start()

    def own_state(t):
        return (tree >> t) & (wide[t] - 1)

    def state_copies(r):
        low, count = rounds[r]
        at = states[low].at[own_state(low)]
        return [
            remote(at, at, state_send.at[n], state_recv.at[n], {"leaf": peer})
            for n, (first, _, peer) in enumerate(peers)
            if first == low
        ]

    def merge(t, node, to):
        both = jnp.concatenate([states[t][2 * node], states[t][2 * node + 1]], axis=1)
        states[t + 1][to, 0:features] = dot(both[0:features], hots[t][node]).astype(BF)
        states[t + 1][to, features:] = dot(both[features:], bases[t][node], 1, 1).astype(BF)

    def far_term(t):
        mine = states[t][own_state(t), 0:features]
        other = states[t][own_state(t) ^ 1]
        other_coords = other[0:features]
        block = tile(
            jnp.transpose(column_form(other_coords, norm_parts(other_coords))),
            row_form(mine, norm_parts(mine)),
            scale,
        )
        far_own[t] = dot(other[features:], block)

    lax.fori_loop(0, leaves, own_columns, 0, unroll=4)
    signs[3 * leaves] = jnp.zeros_like(signs[3 * leaves])
    weights[3 * leaves] = jnp.zeros_like(weights[3 * leaves])
    leaf_columns[3 * leaves] = jnp.zeros_like(leaf_columns[3 * leaves])
    skel_columns[3 * leaves] = jnp.zeros_like(skel_columns[3 * leaves])
    for k in range(1, 4):
        node_copy(k).wait_recv()
    group = jnp.concatenate([nodes[s] for s in range(4)], axis=1)
    states[0][own_state(0), 0:features] = dot(
        group[0:features], one_hot(group.shape[1], subtree_skel[...])
    ).astype(BF)
    states[0][own_state(0), features:] = dot(group[features:], subtree_basis[0], 1, 1).astype(BF)

    half = leaves // 2

    def part_a():
        for copy in basis_copies:
            copy.wait_recv()
        for t in range(levels - 1):
            for node in range(wide[t] // 2):
                hots[t][node] = one_hot(2 * 128, skels[t][node])
        pass_on(5, 6, 0, 1)

    def part_b():
        for t in range(rounds[0][1]):
            far_term(t)
        self_blocks(0, half)
        pass_on(2, 3)
        columns_of(0, 0, half)
        pass_on(4, 7)

    def part_c():
        columns_of(0, half, half)
        self_blocks(half, half)
        pack_queues()
        for t in range(rounds[0][1], rounds[-1][0]):
            far_term(t)
        passed_copy(5).wait_recv()
        for k in range(4):
            passed_copy(k).wait_recv()
            columns_of(1, k * quarter, quarter)

    gaps = [part_a, part_b, part_c]
    for r, (low, count) in enumerate(rounds):
        copies = state_copies(r)
        for copy in copies:
            copy.start()
        gaps[r]()
        for copy in copies:
            copy.wait_recv()
        for t in range(low, min(low + count, levels - 1)):
            if t + 1 < low + count:
                for node in range(wide[t] // 2):
                    merge(t, node, node)
            else:
                merge(t, 0, own_state(t + 1))
    for gap in gaps[len(rounds) :]:
        gap()
    for t in range(rounds[-1][0], levels):
        far_term(t)
    potential = far_own[levels - 1]
    for t in range(levels - 2, -1, -1):
        lane = pl.ds(pl.multiple_of(((tree >> t) & 1) * 128, 128), 128)
        held = (tree >> (t + 1)) & (wide[t] // 2 - 1)
        potential = far_own[t] + dot(potential.astype(BF), bases[t][held, :, lane])
    lane = pl.ds(pl.multiple_of(place * 128, 128), 128)
    potential = dot(potential.astype(BF), subtree_basis[0, :, lane])
    spread[...] = dot(potential.astype(BF), device_basis[0]).astype(BF)

    def tree_step(leaf, _):
        lane = pl.ds(pl.multiple_of(leaf * 128, 128), 128)
        base[leaf] = base[leaf] + dot(spread[:, lane], leaf_basis[leaf])
        return 0

    lax.fori_loop(0, leaves, tree_step, 0, unroll=4)
    passed_copy(4).wait_recv()
    passed_copy(7).wait_recv()

    for k in range(8):
        own_copy(k).wait_send()
        passed_copy(k).wait_send()
    for k in range(1, 4):
        node_copy(k).wait_send()
    for copy in basis_copies:
        copy.wait_send()
    for r in range(len(rounds)):
        for copy in state_copies(r):
            copy.wait_send()
    pltpu.make_async_copy(packed, queues, queue_sem.at[0]).wait()


def pair_kernel(
    leaves,
    features,
    queues,
    leaf_columns,
    leaf_rows,
    skel_columns,
    skel_rows,
    signs,
    weights,
    near_own,
    far_own,
    near_out,
    far_out,
    near_sum,
    far_sum,
    near_tiles,
    far_tiles,
):
    scale = math.log2(math.e) / features
    for total in (near_sum, far_sum):
        total[0 : 2 * leaves] = jnp.zeros((2 * leaves,) + total.shape[1:], F32)
        total[3 * leaves] = jnp.zeros(total.shape[1:], F32)

    def run(which, group, columns, rows, vectors, tiles, total, rounded, both_sides):
        groups = (queues[which, 2, 0] + 2 * group - 1) // (2 * group)

        def make_tile(to, u, pair):
            tiles[to, u] = tile(columns[queues[which, 1, pair]], rows[queues[which, 0, pair]], scale)

        def half(make, to, use, source):
            found = []
            for u in range(group):
                inner = queues[which, 0, use * group + u]
                outer = queues[which, 1, use * group + u]
                block = tiles[source, u]
                found.append((inner, dot(vectors[outer], block)))
                if both_sides:
                    found.append((outer, dot(vectors[inner], block, 1, 1)))
                make_tile(to, u, make * group + u)
            for leaf, term in found:
                total[leaf] += term.astype(BF).astype(F32) if rounded else term

        def step(i, _):
            half(2 * i + 1, 1, 2 * i, 0)
            half(jnp.minimum(2 * i + 2, QUEUE // group - 1), 0, 2 * i + 1, 1)
            return 0

        for u in range(group):
            make_tile(0, u, u)
        lax.fori_loop(0, groups, step, 0)

    for side in range(2):
        run(
            2 + side,
            FAR_GROUPS[side],
            skel_columns,
            skel_rows,
            weights,
            far_tiles,
            far_sum,
            True,
            side == 0,
        )
        run(
            side,
            NEAR_GROUPS[side],
            leaf_columns,
            leaf_rows,
            signs,
            near_tiles,
            near_sum,
            False,
            side == 0,
        )
    near_own[...] = near_sum[0:leaves]
    far_own[...] = far_sum[0:leaves]
    near_out[...] = near_sum[leaves : 2 * leaves].astype(BF)
    far_out[...] = far_sum[leaves : 2 * leaves].astype(BF)


def return_kernel(
    near_own,
    far_leaf,
    near_out,
    far_out,
    base,
    leaf_basis,
    product,
    near_in,
    far_in,
    send_sem,
    recv_sem,
):
    leaves = near_own.shape[0]
    place = lax.axis_index("sub")
    odd = lax.axis_index("leaf") & 1
    ahead = (place + 1 + 2 * odd) & 3
    behind = (place + 3 - 2 * odd) & 3
    barrier = pltpu.get_barrier_semaphore()
    for neighbour in (ahead, behind):
        pl.semaphore_signal(barrier, inc=1, device_id={"sub": neighbour}, device_id_type=MESH)
    pl.semaphore_wait(barrier, 2)

    def copy(k):
        source, target = (near_out, near_in) if k else (far_out, far_in)
        return pltpu.make_async_remote_copy(
            src_ref=source,
            dst_ref=target,
            send_sem=send_sem.at[k],
            recv_sem=recv_sem.at[k],
            device_id={"sub": ahead},
            device_id_type=MESH,
        )

    for k in range(2):
        copy(k).start()
    for k in range(2):
        copy(k).wait_recv()

    def last_step(leaf, _):
        far = far_leaf[leaf] + far_in[leaf].astype(F32)
        high = far.astype(BF)
        low = (far - high.astype(F32)).astype(BF)
        both = dot(jnp.concatenate([high, low], axis=0), leaf_basis[leaf])
        near = near_own[leaf] + near_in[leaf].astype(F32)
        product[leaf] = base[leaf] + near + both[0:16] + both[16:32]
        return 0

    lax.fori_loop(0, leaves, last_step, 0, unroll=4)
    for k in range(2):
        copy(k).wait_send()


def on_device(
    points,
    probe_bits,
    leaf_skel,
    leaf_basis,
    device_skel,
    device_basis,
    subtree_skel,
    subtree_basis,
    upper_skel,
    upper_basis,
    near_pairs,
    near_count,
    far_pairs,
):
    leaves, features, size = points.shape
    probes = probe_bits.shape[1]
    skeleton = leaf_skel.shape[1]
    levels = upper_basis.shape[1] + 1
    known = 3 * leaves + 1
    limit = 40 << 20
    first_limit = 55 << 20
    wide = widths(levels)
    copies = 2 * sum(wide[t] // 2 - 1 for t in range(levels - 1))
    others = sum((1 << count) - 1 for _, count in plan(levels))
    node = features + probes
    (
        leaf_columns,
        leaf_rows,
        skel_columns,
        skel_rows,
        signs,
        weights,
        base,
        basis_held,
        queues,
    ) = pl.pallas_call(
        functools.partial(upward_kernel, levels),
        out_shape=(
            pltpu.VMEM((known, size, 128), BF),
            pltpu.VMEM((leaves, 128, size), BF),
            pltpu.VMEM((known, skeleton, 128), BF),
            pltpu.VMEM((leaves, 128, skeleton), BF),
            pltpu.VMEM((known, probes, size), BF),
            pltpu.VMEM((known, probes, skeleton), BF),
            pltpu.VMEM((leaves, probes, size), F32),
            pltpu.VMEM(leaf_basis.shape, BF),
            pltpu.SMEM((4, 8, QUEUE), I32),
        ),
        in_specs=[HB] * 11 + [SM, HB],
        out_specs=(VM,) * 8 + (SM,),
        scratch_shapes=[
            pltpu.VMEM(points.shape, BF),
            pltpu.VMEM(probe_bits.shape, I32),
            pltpu.VMEM(leaf_skel.shape, I32),
            pltpu.VMEM(device_skel.shape, I32),
            pltpu.VMEM(device_basis.shape, BF),
            pltpu.VMEM(subtree_skel.shape, I32),
            pltpu.VMEM(subtree_basis.shape, BF),
            pltpu.VMEM((1, 2, near_pairs.shape[1]), I32),
            pltpu.VMEM((1, 2, far_pairs.shape[1]), I32),
            pltpu.VMEM((2, leaves, features, size), BF),
            pltpu.VMEM((2, leaves, skeleton), I32),
            pltpu.VMEM((node, leaves * skeleton), BF),
            pltpu.VMEM((4, node, skeleton), BF),
            pltpu.VMEM((3, 8, 128), I32),
            pltpu.VMEM((4, size, size), BF),
            pltpu.VMEM((4, 8, QUEUE), I32),
            pltpu.VMEM((levels, probes, skeleton), F32),
            pltpu.VMEM((probes, leaves * skeleton), BF),
            [pltpu.VMEM((wide[t], node, skeleton), BF) for t in range(levels)],
            [pltpu.VMEM((wide[t] // 2, skeleton, 2 * skeleton), BF) for t in range(levels - 1)],
            [pltpu.VMEM((wide[t] // 2, 1, skeleton), I32) for t in range(levels - 1)],
            [pltpu.VMEM((wide[t] // 2, 2 * skeleton, skeleton), BF) for t in range(levels - 1)],
            pltpu.SemaphoreType.DMA((10 + 2 * (levels - 1),)),
            pltpu.SemaphoreType.DMA((16,)),
            pltpu.SemaphoreType.DMA((8,)),
            pltpu.SemaphoreType.DMA((8,)),
            pltpu.SemaphoreType.DMA((3,)),
            pltpu.SemaphoreType.DMA((3,)),
            pltpu.SemaphoreType.DMA((others,)),
            pltpu.SemaphoreType.DMA((others,)),
            pltpu.SemaphoreType.DMA((copies,)),
            pltpu.SemaphoreType.DMA((copies,)),
            pltpu.SemaphoreType.DMA((1,)),
        ],
        compiler_params=pltpu.CompilerParams(
            collective_id=1, has_side_effects=True, vmem_limit_bytes=first_limit
        ),
        name="upward",
    )(
        points,
        probe_bits,
        leaf_skel,
        leaf_basis,
        device_skel,
        device_basis,
        subtree_skel,
        subtree_basis,
        jnp.transpose(upper_skel, (1, 0, 2)),
        upper_basis,
        jnp.transpose(near_pairs, (0, 2, 1)),
        near_count,
        jnp.transpose(far_pairs, (0, 2, 1)),
    )
    near_own, far_leaf, near_out, far_out = pl.pallas_call(
        functools.partial(pair_kernel, leaves, features),
        out_shape=(
            pltpu.VMEM((leaves, probes, size), F32),
            pltpu.VMEM((leaves, probes, skeleton), F32),
            pltpu.VMEM((leaves, probes, size), BF),
            pltpu.VMEM((leaves, probes, skeleton), BF),
        ),
        in_specs=[SM] + [VM] * 6,
        out_specs=(VM,) * 4,
        scratch_shapes=[
            pltpu.VMEM((known, probes, size), F32),
            pltpu.VMEM((known, probes, skeleton), F32),
            pltpu.VMEM((2, max(NEAR_GROUPS), size, size), BF),
            pltpu.VMEM((2, max(FAR_GROUPS), skeleton, skeleton), BF),
        ],
        compiler_params=pltpu.CompilerParams(vmem_limit_bytes=limit),
        name="pairs",
    )(queues, leaf_columns, leaf_rows, skel_columns, skel_rows, signs, weights)
    return pl.pallas_call(
        return_kernel,
        out_shape=jax.ShapeDtypeStruct((leaves, probes, size), F32),
        in_specs=[VM] * 6,
        out_specs=VM,
        scratch_shapes=[
            pltpu.VMEM((leaves, probes, size), BF),
            pltpu.VMEM((leaves, probes, skeleton), BF),
            pltpu.SemaphoreType.DMA((2,)),
            pltpu.SemaphoreType.DMA((2,)),
        ],
        compiler_params=pltpu.CompilerParams(
            collective_id=2, has_side_effects=True, vmem_limit_bytes=limit
        ),
        name="returned",
    )(near_own, far_leaf, near_out, far_out, base, basis_held)


def solution(mesh):
    return jax.shard_map(
        on_device,
        mesh=mesh,
        in_specs=(
            P(("leaf", "sub"), None, None),
            P(("leaf", "sub"), None, None),
            P(("leaf", "sub"), None),
            P(("leaf", "sub"), None, None),
            P(("leaf", "sub"), None),
            P(("leaf", "sub"), None, None),
            P("leaf", None),
            P("leaf", None, None),
            P("leaf", None, None),
            P("leaf", None, None, None),
            P(("leaf", "sub"), None, None),
            P(("leaf", "sub")),
            P(("leaf", "sub"), None, None),
        ),
        out_specs=P(("leaf", "sub"), None, None),
        check_vma=False,
    )
```

time: 83.8 us -> 65.7 us (0.78)
  the two profiles are of different devices: /device:TPU:56 before, /device:TPU:8 now
where the time goes in v2:
time: 65.7 us; the launch traced here: 65.6 us
  Pallas kernels  64.2 us (98%)
  local copies, waits for them, and re-layouts  0.71 us (1%)
  between operations  0.68 us (1%)
    pallas_call x1, Pallas kernels, on_device(): pl.pallas_call(functools.partial(upward_kernel, levels), out_shape=(pltpu...  42.6 us
    pallas_call x1, Pallas kernels, on_device(): pl.pallas_call(return_kernel, out_shape=jax.ShapeDtypeStruct((leaves, pro...  11.6 us
    pallas_call x1, Pallas kernels, on_device(): pl.pallas_call(functools.partial(pair_kernel, leaves, features), out_shap...  9.94 us

profile of v2, /device:TPU:8, one launch (start us, length us, event | category | flops | bytes accessed | tf_op | source)
XLA Modules:
  0.0 65.6 jit_solution(12834625802062800198)
XLA Ops:
  0.7 42.6 %upward.1 = (bf16[49,256,128]{2,1,0:T(8,128)(2,1)S(1)}, bf16[16,128,256]{2,1,0:T(8,128)(2,1)S(1)}, bf16[49,128,128]{2,1,0:T(8,128)(2,1)S(1)}, bf16[16,128,128]{2...) custom-call(bf16[16,64,256]{2,1,0:T(8,128)(2,1)} %points_in.1, ...), custom_call_target="tpu_custom_call" | custom-call | tf_op jit(solution)/shard_map/upward/pallas_call | solution.py:653
  43.3 9.9 %pairs.1 = (f32[16,16,256]{2,1,0:T(8,128)S(1)}, f32[16,16,128]{2,1,0:T(8,128)S(1)}, bf16[16,16,256]{2,1,0:T(8,128)(2,1)S(1)}, bf16[16,16,128]{2,1,0:T(8,128)(2,1)S(1)}) custom-call(s32[4,8,240]{2,1,0:T(8,128)S(4)} %get-tuple-element.18.queues, bf16[49,256,128]{2,1,0:T(8,128)(2,1)S(1)} %get-tuple-element.19.leaf_columns, ...), custom_call_target="tpu_custom_call" | custom-call | tf_op jit(solution)/shard_map/pairs/pallas_call | solution.py:722
  53.2 11.6 %returned.1 = f32[16,16,256]{2,1,0:T(8,128)S(1)} custom-call(f32[16,16,256]{2,1,0:T(8,128)S(1)} %get-tuple-element.25.near_own, f32[16,16,128]{2,1,0:T(8,128)S(1)} %get-tuple-element.26.far_leaf, bf16[16,16,256]{2,1,0:T(8,128)(2,1)S(1)} %get-tuple-element.27.near_out, bf16[16,16,128]{2,1,0:T(8,128)(2,1)S(1)} %get-tuple-element.28.far_out, ...), custom_call_target="tpu_custom_call" | custom-call | tf_op jit(solution)/shard_map/returned/pallas_call | solution.py:741
  64.9 0.7 %copy.16 = f32[16,16,256]{2,1,0:T(8,128)} copy(f32[16,16,256]{2,1,0:T(8,128)S(1)} %returned.1) | data formatting | bytes 524288

commit v3 on v2

--- a/solution.py
+++ b/solution.py
@@ -15,8 +15,8 @@
 VM = pl.BlockSpec(memory_space=pltpu.VMEM)
 SM = pl.BlockSpec(memory_space=pltpu.SMEM)
 HB = pl.BlockSpec(memory_space=pltpu.HBM)
-NEAR_GROUPS = (6, 4)
-FAR_GROUPS = (12, 8)
+NEAR_GROUP, FAR_GROUP = 6, 12
+NEAR_FIXED, FAR_FIXED = (48, 24), (72, 48)
 QUEUE = 240
 
 
@@ -76,6 +76,56 @@
 
 def widths(levels):
     return [1 << (low + count - t) for low, count in plan(levels) for t in range(low, low + count)]
+
+
+def far_between(mine, other, features):
+    coords, other_coords = mine[0:features], other[0:features]
+    block = tile(
+        jnp.transpose(column_form(other_coords, norm_parts(other_coords))),
+        row_form(coords, norm_parts(coords)),
+        math.log2(math.e) / features,
+    )
+    return dot(other[features:], block)
+
+
+def pair_groups(
+    queues, which, group, first, groups, tables, tiles, scale, rounded, both_sides, emit
+):
+    columns, rows, inner_vectors, outer_vectors = tables
+
+    def at(pair):
+        inner = jnp.clip(queues[which, 0, pair], 0, rows.shape[0] - 1)
+        outer = jnp.clip(queues[which, 1, pair], 0, columns.shape[0] - 1)
+        return inner, outer
+
+    def make_tile(to, u, pair):
+        inner, outer = at(pair)
+        tiles[to, u] = tile(columns[outer], rows[inner], scale)
+
+    def half(make, to, use, source):
+        found = []
+        for u in range(group):
+            pair = first + use * group + u
+            inner, outer = at(pair)
+            block = tiles[source, u]
+            terms = [dot(outer_vectors[outer], block)]
+            if both_sides:
+                terms.append(dot(inner_vectors[inner], block, 1, 1))
+            if rounded:
+                terms = [term.astype(BF).astype(F32) for term in terms]
+            found.append((pair, inner, outer, terms[0], terms[-1]))
+            make_tile(to, u, first + make * group + u)
+        for one in found:
+            emit(*one)
+
+    def step(i, _):
+        half(2 * i + 1, 1, 2 * i, 0)
+        half(jnp.minimum(2 * i + 2, (QUEUE - first) // group - 1), 0, 2 * i + 1, 1)
+        return 0
+
+    for u in range(group):
+        make_tile(0, u, first + u)
+    lax.fori_loop(0, groups, step, 0)
 
 
 def upward_kernel(
@@ -94,21 +144,30 @@
     near_count,
     far_in,
     leaf_columns,
+    far_leaf_columns,
     leaf_rows,
     skel_columns,
+    far_skel_columns,
     skel_rows,
     signs,
+    far_signs,
     weights,
+    far_weights,
+    near_terms,
+    far_terms,
     base,
     leaf_basis,
+    device_basis,
+    subtree_basis,
+    upper_basis,
+    far_own,
+    last_pairs,
     queues,
     points,
     bits,
     leaf_skel,
     device_skel,
-    device_basis,
     subtree_skel,
-    subtree_basis,
     near_pairs,
     far_pairs,
     far_points,
@@ -116,10 +175,9 @@
     joined,
     nodes,
     lists,
-    tiles,
+    near_tiles,
+    far_tiles,
     packed,
-    far_own,
-    spread,
     states,
     bases,
     skels,
@@ -170,6 +228,7 @@
         held = (tree >> (t + 1)) & (wide[t] // 2 - 1)
         loads.append((upper_basis_in.at[0, t], bases[t].at[held]))
         loads.append((upper_skel_in.at[t], skels[t].at[held]))
+    loads.append((upper_basis_in, upper_basis))
 
     def load(k):
         return pltpu.make_async_copy(loads[k][0], loads[k][1], load_sem.at[k])
@@ -191,7 +250,7 @@
     lists[0, 2:4, 0 : far_pairs.shape[2]] = far_pairs[0]
     lists[0, 4:5, :] = jnp.full((1, 128), near_count[0], I32)
 
-    for k in range(3, len(loads)):
+    for k in range(3, len(loads) - 1):
         load(k).wait()
 
     def leaf_step(leaf, _):
@@ -241,16 +300,16 @@
             part = pl.ds(k * quarter, quarter)
             pair = (far_points.at[0, part], far_points.at[1, part])
         elif k == 4:
-            pair = (signs.at[pl.ds(leaves, leaves)], signs.at[pl.ds(2 * leaves, leaves)])
+            pair = (signs.at[pl.ds(leaves, leaves)], far_signs.at[pl.ds(0, leaves)])
         elif k == 5:
             pair = (far_skel.at[0], far_skel.at[1])
         elif k == 6:
             pair = (lists.at[1], lists.at[2])
         else:
-            pair = (weights.at[pl.ds(leaves, leaves)], weights.at[pl.ds(2 * leaves, leaves)])
+            pair = (weights.at[pl.ds(leaves, leaves)], far_weights.at[pl.ds(0, leaves)])
         return remote(*pair, send_sem.at[8 + k], pass_sem.at[k], {"sub": behind})
 
-    for k in (5, 6, 0, 1, 2, 3, 4, 7):
+    for k in (5, 6, 4, 7, 0, 1, 2, 3):
         own_copy(k).start()
 
     nodes[place, 0:features] = dot(
@@ -295,12 +354,15 @@
         return 0
 
     def columns_of(slot, first, count):
+        leaf_to, skel_to = (far_leaf_columns, far_skel_columns) if slot else (leaf_columns, skel_columns)
+        leaf_at = 0 if slot else leaves
+
         def step(leaf, _):
             coords = far_points[slot, leaf]
             columns = column_form(coords, norm_parts(coords))
-            leaf_columns[(slot + 1) * leaves + leaf] = jnp.transpose(columns)
+            leaf_to[leaf_at + leaf] = jnp.transpose(columns)
             picked = dot(columns, one_hot(size, far_skel[slot, pl.ds(leaf, 1), :])).astype(BF)
-            skel_columns[(slot + 1) * leaves + leaf] = jnp.transpose(picked)
+            skel_to[leaf_at + leaf] = jnp.transpose(picked)
             return 0
 
         lax.fori_loop(first, first + count, step, 0, unroll=4)
@@ -309,9 +371,9 @@
         def step(i, _):
             at = first + 4 * i
             for u in range(4):
-                tiles[u] = tile(leaf_columns[at + u], leaf_rows[at + u], scale)
+                near_tiles[0, u] = tile(leaf_columns[at + u], leaf_rows[at + u], scale)
             for u in range(4):
-                base[at + u] = dot(signs[at + u], tiles[u])
+                base[at + u] = dot(signs[at + u], near_tiles[0, u])
             return 0
 
         lax.fori_loop(0, count // 4, step, 0)
@@ -339,15 +401,16 @@
             holder = second >> 4
             slot = ((holder - place) * (1 + 2 * odd)) & 3
             inner = jnp.where(origin == 0, first, second & 15)
-            outer = jnp.where(origin == 0, slot, origin) * 16
-            outer = outer + jnp.where(origin == 0, second & 15, first) - 48
+            outer = jnp.where(origin == 0, second & 15, first)
+            spread_out = jnp.where(origin == 0, slot, origin) * 16 + outer - 32
             here = jnp.where(slot == 0, 1, 0)
             both_sides = jnp.where(origin == 0, jnp.where(slot < 2, 1, 0), jnp.where(origin == 1, here, 0))
             one_side = jnp.where(
                 origin == 0, jnp.where(slot == 2, 1, 0), jnp.where(origin == 2, here, 0)
             )
-            codes = jnp.where(eight == 0, inner, outer).astype(F32).astype(BF)
             for side, wanted in enumerate((both_sides, one_side)):
+                code = outer - 16 if side else spread_out
+                codes = jnp.where(eight == 0, inner, code).astype(F32).astype(BF)
                 keep = jnp.where(spot < count, wanted, 0)
                 keep_f = jnp.where(keep == 1, 1.0, 0.0)
                 total = jnp.sum(keep_f, axis=1, keepdims=True)
@@ -357,7 +420,7 @@
                     lax.broadcasted_iota(I32, (QUEUE, 384), 0).astype(F32) == rank, 1.0, 0.0
                 ).astype(BF)
                 taken = dot(codes, chosen, 1, 1)
-                taken = jnp.where(eight_out == 0, taken, taken + 48.0)
+                taken = jnp.where(eight_out == 0, taken, taken + (16.0 if side else 32.0))
                 packed[which + side] = jnp.where(eight_out == 2, total, taken).astype(I32)
         pltpu.make_async_copy(packed, queues, queue_sem.at[0]).start()
 
@@ -379,21 +442,17 @@
         states[t + 1][to, features:] = dot(both[features:], bases[t][node], 1, 1).astype(BF)
 
     def far_term(t):
-        mine = states[t][own_state(t), 0:features]
-        other = states[t][own_state(t) ^ 1]
-        other_coords = other[0:features]
-        block = tile(
-            jnp.transpose(column_form(other_coords, norm_parts(other_coords))),
-            row_form(mine, norm_parts(mine)),
-            scale,
-        )
-        far_own[t] = dot(other[features:], block)
+        far_own[t] = far_between(states[t][own_state(t)], states[t][own_state(t) ^ 1], features)
 
     lax.fori_loop(0, leaves, own_columns, 0, unroll=4)
-    signs[3 * leaves] = jnp.zeros_like(signs[3 * leaves])
-    weights[3 * leaves] = jnp.zeros_like(weights[3 * leaves])
-    leaf_columns[3 * leaves] = jnp.zeros_like(leaf_columns[3 * leaves])
-    skel_columns[3 * leaves] = jnp.zeros_like(skel_columns[3 * leaves])
+    signs[2 * leaves] = jnp.zeros_like(signs[2 * leaves])
+    far_signs[leaves] = jnp.zeros_like(far_signs[leaves])
+    weights[2 * leaves] = jnp.zeros_like(weights[2 * leaves])
+    far_weights[leaves] = jnp.zeros_like(far_weights[leaves])
+    leaf_columns[2 * leaves] = jnp.zeros_like(leaf_columns[2 * leaves])
+    far_leaf_columns[leaves] = jnp.zeros_like(far_leaf_columns[leaves])
+    skel_columns[2 * leaves] = jnp.zeros_like(skel_columns[2 * leaves])
+    far_skel_columns[leaves] = jnp.zeros_like(far_skel_columns[leaves])
     for k in range(1, 4):
         node_copy(k).wait_recv()
     group = jnp.concatenate([nodes[s] for s in range(4)], axis=1)
@@ -402,34 +461,70 @@
     ).astype(BF)
     states[0][own_state(0), features:] = dot(group[features:], subtree_basis[0], 1, 1).astype(BF)
 
-    half = leaves // 2
-
     def part_a():
         for copy in basis_copies:
             copy.wait_recv()
         for t in range(levels - 1):
             for node in range(wide[t] // 2):
                 hots[t][node] = one_hot(2 * 128, skels[t][node])
-        pass_on(5, 6, 0, 1)
+        self_blocks(0, quarter)
+        pass_on(5, 6, 4, 7)
 
     def part_b():
         for t in range(rounds[0][1]):
             far_term(t)
-        self_blocks(0, half)
-        pass_on(2, 3)
-        columns_of(0, 0, half)
-        pass_on(4, 7)
+        self_blocks(quarter, leaves - quarter)
+        for k in range(2):
+            pass_on(k)
+            columns_of(0, k * quarter, quarter)
+
+    def fixed_pairs(side):
+        outer_signs, outer_weights = (far_signs, far_weights) if side else (signs, weights)
+        outer_leaf, outer_skel = (
+            (far_leaf_columns, far_skel_columns) if side else (leaf_columns, skel_columns)
+        )
+        for which, group, fixed, terms, rounded, tables, tiles in (
+            (2, FAR_GROUP, FAR_FIXED, far_terms, True, (outer_skel, skel_rows, weights, outer_weights), far_tiles),
+            (0, NEAR_GROUP, NEAR_FIXED, near_terms, False, (outer_leaf, leaf_rows, signs, outer_signs), near_tiles),
+        ):
+
+            def emit(pair, inner, outer, to_inner, to_outer):
+                if side:
+                    terms[2 * fixed[0] + pair] = to_inner
+                else:
+                    terms[2 * pair] = to_inner
+                    terms[2 * pair + 1] = to_outer
+
+            pair_groups(
+                queues,
+                which + side,
+                group,
+                0,
+                fixed[side] // (2 * group),
+                tables,
+                tiles,
+                scale,
+                rounded,
+                side == 0,
+                emit,
+            )
 
     def part_c():
-        columns_of(0, half, half)
-        self_blocks(half, half)
         pack_queues()
+        for k in range(2, 4):
+            pass_on(k)
+            columns_of(0, k * quarter, quarter)
         for t in range(rounds[0][1], rounds[-1][0]):
             far_term(t)
+        pltpu.make_async_copy(packed, queues, queue_sem.at[0]).wait()
+        fixed_pairs(0)
         passed_copy(5).wait_recv()
         for k in range(4):
             passed_copy(k).wait_recv()
             columns_of(1, k * quarter, quarter)
+        passed_copy(4).wait_recv()
+        passed_copy(7).wait_recv()
+        fixed_pairs(1)
 
     gaps = [part_a, part_b, part_c]
     for r, (low, count) in enumerate(rounds):
@@ -448,25 +543,8 @@
     for gap in gaps[len(rounds) :]:
         gap()
     for t in range(rounds[-1][0], levels):
-        far_term(t)
-    potential = far_own[levels - 1]
-    for t in range(levels - 2, -1, -1):
-        lane = pl.ds(pl.multiple_of(((tree >> t) & 1) * 128, 128), 128)
-        held = (tree >> (t + 1)) & (wide[t] // 2 - 1)
-        potential = far_own[t] + dot(potential.astype(BF), bases[t][held, :, lane])
-    lane = pl.ds(pl.multiple_of(place * 128, 128), 128)
-    potential = dot(potential.astype(BF), subtree_basis[0, :, lane])
-    spread[...] = dot(potential.astype(BF), device_basis[0]).astype(BF)
-
-    def tree_step(leaf, _):
-        lane = pl.ds(pl.multiple_of(leaf * 128, 128), 128)
-        base[leaf] = base[leaf] + dot(spread[:, lane], leaf_basis[leaf])
-        return 0
-
-    lax.fori_loop(0, leaves, tree_step, 0, unroll=4)
-    passed_copy(4).wait_recv()
-    passed_copy(7).wait_recv()
-
+        for other in range(2):
+            last_pairs[t - rounds[-1][0], other] = states[t][own_state(t) ^ other]
     for k in range(8):
         own_copy(k).wait_send()
         passed_copy(k).wait_send()
@@ -477,7 +555,7 @@
     for r in range(len(rounds)):
         for copy in state_copies(r):
             copy.wait_send()
-    pltpu.make_async_copy(packed, queues, queue_sem.at[0]).wait()
+    load(len(loads) - 1).wait()
 
 
 def pair_kernel(
@@ -485,11 +563,17 @@
     features,
     queues,
     leaf_columns,
+    far_leaf_columns,
     leaf_rows,
     skel_columns,
+    far_skel_columns,
     skel_rows,
     signs,
+    far_signs,
     weights,
+    far_weights,
+    near_terms,
+    far_terms,
     near_own,
     far_own,
     near_out,
@@ -500,61 +584,57 @@
     far_tiles,
 ):
     scale = math.log2(math.e) / features
-    for total in (near_sum, far_sum):
-        total[0 : 2 * leaves] = jnp.zeros((2 * leaves,) + total.shape[1:], F32)
-        total[3 * leaves] = jnp.zeros(total.shape[1:], F32)
-
-    def run(which, group, columns, rows, vectors, tiles, total, rounded, both_sides):
-        groups = (queues[which, 2, 0] + 2 * group - 1) // (2 * group)
-
-        def make_tile(to, u, pair):
-            tiles[to, u] = tile(columns[queues[which, 1, pair]], rows[queues[which, 0, pair]], scale)
-
-        def half(make, to, use, source):
-            found = []
-            for u in range(group):
-                inner = queues[which, 0, use * group + u]
-                outer = queues[which, 1, use * group + u]
-                block = tiles[source, u]
-                found.append((inner, dot(vectors[outer], block)))
+    near_sum[...] = jnp.zeros_like(near_sum)
+    far_sum[...] = jnp.zeros_like(far_sum)
+    steps = math.gcd(*NEAR_FIXED, *FAR_FIXED)
+
+    def add_fixed(i, _):
+        for which, fixed, terms, total in (
+            (0, NEAR_FIXED, near_terms, near_sum),
+            (2, FAR_FIXED, far_terms, far_sum),
+        ):
+            share = fixed[0] // steps
+            for u in range(share):
+                pair = i * share + u
+                total[queues[which, 0, pair]] += terms[2 * pair]
+                total[queues[which, 1, pair]] += terms[2 * pair + 1]
+            share = fixed[1] // steps
+            for u in range(share):
+                pair = i * share + u
+                total[queues[which + 1, 0, pair]] += terms[2 * fixed[0] + pair]
+        return 0
+
+    lax.fori_loop(0, steps, add_fixed, 0)
+    for which, group, fixed, total, rounded, tables, tiles in (
+        (2, FAR_GROUP, FAR_FIXED[0], far_sum, True, (skel_columns, skel_rows, weights, weights), far_tiles),
+        (3, FAR_GROUP, FAR_FIXED[1], far_sum, True, (far_skel_columns, skel_rows, weights, far_weights), far_tiles),
+        (0, NEAR_GROUP, NEAR_FIXED[0], near_sum, False, (leaf_columns, leaf_rows, signs, signs), near_tiles),
+        (1, NEAR_GROUP, NEAR_FIXED[1], near_sum, False, (far_leaf_columns, leaf_rows, signs, far_signs), near_tiles),
+    ):
+        both_sides = which % 2 == 0
+        left = queues[which, 2, 0] - fixed
+
+        @pl.when(left > 0)
+        def _():
+            def emit(pair, inner, outer, to_inner, to_outer):
+                total[inner] += to_inner
                 if both_sides:
-                    found.append((outer, dot(vectors[inner], block, 1, 1)))
-                make_tile(to, u, make * group + u)
-            for leaf, term in found:
-                total[leaf] += term.astype(BF).astype(F32) if rounded else term
-
-        def step(i, _):
-            half(2 * i + 1, 1, 2 * i, 0)
-            half(jnp.minimum(2 * i + 2, QUEUE // group - 1), 0, 2 * i + 1, 1)
-            return 0
-
-        for u in range(group):
-            make_tile(0, u, u)
-        lax.fori_loop(0, groups, step, 0)
-
-    for side in range(2):
-        run(
-            2 + side,
-            FAR_GROUPS[side],
-            skel_columns,
-            skel_rows,
-            weights,
-            far_tiles,
-            far_sum,
-            True,
-            side == 0,
-        )
-        run(
-            side,
-            NEAR_GROUPS[side],
-            leaf_columns,
-            leaf_rows,
-            signs,
-            near_tiles,
-            near_sum,
-            False,
-            side == 0,
-        )
+                    total[outer] += to_outer
+
+            pair_groups(
+                queues,
+                which,
+                group,
+                fixed,
+                (left + 2 * group - 1) // (2 * group),
+                tables,
+                tiles,
+                scale,
+                rounded,
+                both_sides,
+                emit,
+            )
+
     near_own[...] = near_sum[0:leaves]
     far_own[...] = far_sum[0:leaves]
     near_out[...] = near_sum[leaves : 2 * leaves].astype(BF)
@@ -562,21 +642,30 @@
 
 
 def return_kernel(
+    levels,
+    features,
     near_own,
     far_leaf,
     near_out,
     far_out,
     base,
     leaf_basis,
+    device_basis,
+    subtree_basis,
+    upper_basis,
+    far_own,
+    last_pairs,
     product,
     near_in,
     far_in,
+    spread,
     send_sem,
     recv_sem,
 ):
     leaves = near_own.shape[0]
     place = lax.axis_index("sub")
-    odd = lax.axis_index("leaf") & 1
+    tree = lax.axis_index("leaf")
+    odd = tree & 1
     ahead = (place + 1 + 2 * odd) & 3
     behind = (place + 3 - 2 * odd) & 3
     barrier = pltpu.get_barrier_semaphore()
@@ -597,6 +686,26 @@
 
     for k in range(2):
         copy(k).start()
+
+    first = levels - last_pairs.shape[0]
+    fars = [far_own[t] for t in range(first)]
+    for t in range(first, levels):
+        fars.append(far_between(last_pairs[t - first, 0], last_pairs[t - first, 1], features))
+    potential = fars[levels - 1]
+    for t in range(levels - 2, -1, -1):
+        lane = pl.ds(pl.multiple_of(((tree >> t) & 1) * 128, 128), 128)
+        potential = fars[t] + dot(potential.astype(BF), upper_basis[0, t, :, lane])
+    lane = pl.ds(pl.multiple_of(place * 128, 128), 128)
+    potential = dot(potential.astype(BF), subtree_basis[0, :, lane])
+    spread[...] = dot(potential.astype(BF), device_basis[0]).astype(BF)
+
+    def tree_step(leaf, _):
+        lane = pl.ds(pl.multiple_of(leaf * 128, 128), 128)
+        near = base[leaf] + near_own[leaf]
+        product[leaf] = near + dot(spread[:, lane], leaf_basis[leaf])
+        return 0
+
+    lax.fori_loop(0, leaves, tree_step, 0, unroll=4)
     for k in range(2):
         copy(k).wait_recv()
 
@@ -605,8 +714,8 @@
         high = far.astype(BF)
         low = (far - high.astype(F32)).astype(BF)
         both = dot(jnp.concatenate([high, low], axis=0), leaf_basis[leaf])
-        near = near_own[leaf] + near_in[leaf].astype(F32)
-        product[leaf] = base[leaf] + near + both[0:16] + both[16:32]
+        near = product[leaf] + near_in[leaf].astype(F32)
+        product[leaf] = near + both[0:16] + both[16:32]
         return 0
 
     lax.fori_loop(0, leaves, last_step, 0, unroll=4)
@@ -633,46 +742,46 @@
     probes = probe_bits.shape[1]
     skeleton = leaf_skel.shape[1]
     levels = upper_basis.shape[1] + 1
-    known = 3 * leaves + 1
-    limit = 40 << 20
-    first_limit = 55 << 20
+    known = 2 * leaves + 1
+    beyond = leaves + 1
+    limit = 32 << 20
+    first_limit = 50 << 20
     wide = widths(levels)
     copies = 2 * sum(wide[t] // 2 - 1 for t in range(levels - 1))
     others = sum((1 << count) - 1 for _, count in plan(levels))
     node = features + probes
-    (
-        leaf_columns,
-        leaf_rows,
-        skel_columns,
-        skel_rows,
-        signs,
-        weights,
-        base,
-        basis_held,
-        queues,
-    ) = pl.pallas_call(
+    outs = pl.pallas_call(
         functools.partial(upward_kernel, levels),
         out_shape=(
             pltpu.VMEM((known, size, 128), BF),
+            pltpu.VMEM((beyond, size, 128), BF),
             pltpu.VMEM((leaves, 128, size), BF),
             pltpu.VMEM((known, skeleton, 128), BF),
+            pltpu.VMEM((beyond, skeleton, 128), BF),
             pltpu.VMEM((leaves, 128, skeleton), BF),
             pltpu.VMEM((known, probes, size), BF),
+            pltpu.VMEM((beyond, probes, size), BF),
             pltpu.VMEM((known, probes, skeleton), BF),
+            pltpu.VMEM((beyond, probes, skeleton), BF),
+            pltpu.VMEM((2 * NEAR_FIXED[0] + NEAR_FIXED[1], probes, size), F32),
+            pltpu.VMEM((2 * FAR_FIXED[0] + FAR_FIXED[1], probes, skeleton), F32),
             pltpu.VMEM((leaves, probes, size), F32),
             pltpu.VMEM(leaf_basis.shape, BF),
+            pltpu.VMEM(device_basis.shape, BF),
+            pltpu.VMEM(subtree_basis.shape, BF),
+            pltpu.VMEM(upper_basis.shape, BF),
+            pltpu.VMEM((levels, probes, skeleton), F32),
+            pltpu.VMEM((plan(levels)[-1][1], 2, node, skeleton), BF),
             pltpu.SMEM((4, 8, QUEUE), I32),
         ),
         in_specs=[HB] * 11 + [SM, HB],
-        out_specs=(VM,) * 8 + (SM,),
+        out_specs=(VM,) * 19 + (SM,),
         scratch_shapes=[
             pltpu.VMEM(points.shape, BF),
             pltpu.VMEM(probe_bits.shape, I32),
             pltpu.VMEM(leaf_skel.shape, I32),
             pltpu.VMEM(device_skel.shape, I32),
-            pltpu.VMEM(device_basis.shape, BF),
             pltpu.VMEM(subtree_skel.shape, I32),
-            pltpu.VMEM(subtree_basis.shape, BF),
             pltpu.VMEM((1, 2, near_pairs.shape[1]), I32),
             pltpu.VMEM((1, 2, far_pairs.shape[1]), I32),
             pltpu.VMEM((2, leaves, features, size), BF),
@@ -680,15 +789,14 @@
             pltpu.VMEM((node, leaves * skeleton), BF),
             pltpu.VMEM((4, node, skeleton), BF),
             pltpu.VMEM((3, 8, 128), I32),
-            pltpu.VMEM((4, size, size), BF),
+            pltpu.VMEM((2, NEAR_GROUP, size, size), BF),
+            pltpu.VMEM((2, FAR_GROUP, skeleton, skeleton), BF),
             pltpu.VMEM((4, 8, QUEUE), I32),
-            pltpu.VMEM((levels, probes, skeleton), F32),
-            pltpu.VMEM((probes, leaves * skeleton), BF),
             [pltpu.VMEM((wide[t], node, skeleton), BF) for t in range(levels)],
             [pltpu.VMEM((wide[t] // 2, skeleton, 2 * skeleton), BF) for t in range(levels - 1)],
             [pltpu.VMEM((wide[t] // 2, 1, skeleton), I32) for t in range(levels - 1)],
             [pltpu.VMEM((wide[t] // 2, 2 * skeleton, skeleton), BF) for t in range(levels - 1)],
-            pltpu.SemaphoreType.DMA((10 + 2 * (levels - 1),)),
+            pltpu.SemaphoreType.DMA((11 + 2 * (levels - 1),)),
             pltpu.SemaphoreType.DMA((16,)),
             pltpu.SemaphoreType.DMA((8,)),
             pltpu.SemaphoreType.DMA((8,)),
@@ -719,6 +827,7 @@
         near_count,
         jnp.transpose(far_pairs, (0, 2, 1)),
     )
+    pair_tables, passed_on, queues = outs[:12], outs[12:19], outs[19]
     near_own, far_leaf, near_out, far_out = pl.pallas_call(
         functools.partial(pair_kernel, leaves, features),
         out_shape=(
@@ -727,25 +836,26 @@
             pltpu.VMEM((leaves, probes, size), BF),
             pltpu.VMEM((leaves, probes, skeleton), BF),
         ),
-        in_specs=[SM] + [VM] * 6,
+        in_specs=[SM] + [VM] * 12,
         out_specs=(VM,) * 4,
         scratch_shapes=[
             pltpu.VMEM((known, probes, size), F32),
             pltpu.VMEM((known, probes, skeleton), F32),
-            pltpu.VMEM((2, max(NEAR_GROUPS), size, size), BF),
-            pltpu.VMEM((2, max(FAR_GROUPS), skeleton, skeleton), BF),
+            pltpu.VMEM((2, NEAR_GROUP, size, size), BF),
+            pltpu.VMEM((2, FAR_GROUP, skeleton, skeleton), BF),
         ],
         compiler_params=pltpu.CompilerParams(vmem_limit_bytes=limit),
         name="pairs",
-    )(queues, leaf_columns, leaf_rows, skel_columns, skel_rows, signs, weights)
+    )(queues, *pair_tables)
     return pl.pallas_call(
-        return_kernel,
+        functools.partial(return_kernel, levels, features),
         out_shape=jax.ShapeDtypeStruct((leaves, probes, size), F32),
-        in_specs=[VM] * 6,
+        in_specs=[VM] * 11,
         out_specs=VM,
         scratch_shapes=[
             pltpu.VMEM((leaves, probes, size), BF),
             pltpu.VMEM((leaves, probes, skeleton), BF),
+            pltpu.VMEM((probes, leaves * skeleton), BF),
             pltpu.SemaphoreType.DMA((2,)),
             pltpu.SemaphoreType.DMA((2,)),
         ],
@@ -753,7 +863,7 @@
             collective_id=2, has_side_effects=True, vmem_limit_bytes=limit
         ),
         name="returned",
-    )(near_own, far_leaf, near_out, far_out, base, basis_held)
+    )(near_own, far_leaf, near_out, far_out, *passed_on)
 
 
 def solution(mesh):

time: 65.7 us -> 62 us (0.944)
  the two profiles are of different devices: /device:TPU:8 before, /device:TPU:74 now
where the time goes in v3:
time: 62 us; the launch traced here: 61.8 us
  Pallas kernels  60.4 us (97%)
  local copies, waits for them, and re-layouts  0.71 us (1%)
  between operations  0.68 us (1%)
    pallas_call x1, Pallas kernels, on_device(): pl.pallas_call(functools.partial(upward_kernel, levels), out_shape=(pltpu...  47 us
    pallas_call x1, Pallas kernels, on_device(): pl.pallas_call(functools.partial(return_kernel, levels, features), out_sh...  10.2 us
    pallas_call x1, Pallas kernels, on_device(): pl.pallas_call(functools.partial(pair_kernel, leaves, features), out_shap...  3.19 us

profile of v3, /device:TPU:74, one launch (start us, length us, event | category | flops | bytes accessed | tf_op | source)
XLA Modules:
  0.0 61.8 jit_solution(14783222440748746624)
XLA Ops:
  0.7 47.0 %upward.1 = (bf16[33,256,128]{2,1,0:T(8,128)(2,1)S(1)}, bf16[17,256,128]{2,1,0:T(8,128)(2,1)S(1)}, bf16[16,128,256]{2,1,0:T(8,128)(2,1)S(1)}, bf16[33,128,128]{2...) custom-call(bf16[16,64,256]{2,1,0:T(8,128)(2,1)} %points_in.1, ...), custom_call_target="tpu_custom_call" | custom-call | tf_op jit(solution)/shard_map/upward/pallas_call | solution.py:753
  47.7 3.2 %pairs.1 = (f32[16,16,256]{2,1,0:T(8,128)S(1)}, f32[16,16,128]{2,1,0:T(8,128)S(1)}, bf16[16,16,256]{2,1,0:T(8,128)(2,1)S(1)}, bf16[16,16,128]{2,1,0:T(8,128)(2,1)S(1)}) custom-call(s32[4,8,240]{2,1,0:T(8,128)S(4)} %get-tuple-element.29.queues, bf16[33,256,128]{2,1,0:T(8,128)(2,1)S(1)} %get-tuple-element.30.leaf_columns, ...), custom_call_target="tpu_custom_call" | custom-call | tf_op jit(solution)/shard_map/pairs/pallas_call | solution.py:831
  50.9 10.2 %returned.1 = f32[16,16,256]{2,1,0:T(8,128)S(1)} custom-call(f32[16,16,256]{2,1,0:T(8,128)S(1)} %get-tuple-element.42.near_own, f32[16,16,128]{2,1,0:T(8,128)S(1)} %get-tuple-element.43.far_leaf, bf16[16,16,256]{2,1,0:T(8,128)(2,1)S(1)} %get-tuple-element.44.near_out, bf16[16,16,128]{2,1,0:T(8,128)(2,1)S(1)} %get-tuple-element.45.far_out, ...), custom_call_target="tpu_custom_call" | custom-call | tf_op jit(solution)/shard_map/returned/pallas_call | solution.py:850
  61.1 0.7 %copy.16 = f32[16,16,256]{2,1,0:T(8,128)} copy(f32[16,16,256]{2,1,0:T(8,128)S(1)} %returned.1) | data formatting | bytes 524288

commit v4 on v3

--- a/solution.py
+++ b/solution.py
@@ -114,7 +114,8 @@
             if rounded:
                 terms = [term.astype(BF).astype(F32) for term in terms]
             found.append((pair, inner, outer, terms[0], terms[-1]))
-            make_tile(to, u, first + make * group + u)
+            if make is not None:
+                make_tile(to, u, first + make * group + u)
         for one in found:
             emit(*one)
 
@@ -125,7 +126,12 @@
 
     for u in range(group):
         make_tile(0, u, first + u)
-    lax.fori_loop(0, groups, step, 0)
+    if isinstance(groups, int):
+        lax.fori_loop(0, groups - 1, step, 0)
+        half(2 * groups - 1, 1, 2 * groups - 2, 0)
+        half(None, 0, 2 * groups - 1, 1)
+    else:
+        lax.fori_loop(0, groups, step, 0)
 
 
 def upward_kernel(
@@ -477,6 +483,7 @@
         for k in range(2):
             pass_on(k)
             columns_of(0, k * quarter, quarter)
+        pack_queues()
 
     def fixed_pairs(side):
         outer_signs, outer_weights = (far_signs, far_weights) if side else (signs, weights)
@@ -510,7 +517,6 @@
             )
 
     def part_c():
-        pack_queues()
         for k in range(2, 4):
             pass_on(k)
             columns_of(0, k * quarter, quarter)

time: 62 us -> 58.6 us (0.945)
  the two profiles are of different devices: /device:TPU:74 before, /device:TPU:72 now
where the time goes in v4:
time: 58.6 us
  Pallas kernels  57.2 us (98%)
  local copies, waits for them, and re-layouts  0.71 us (1%)
  between operations  0.68 us (1%)
    pallas_call x1, Pallas kernels, on_device(): pl.pallas_call(functools.partial(upward_kernel, levels), out_shape=(pltpu...  44.5 us
    pallas_call x1, Pallas kernels, on_device(): pl.pallas_call(functools.partial(return_kernel, levels, features), out_sh...  9.31 us
    pallas_call x1, Pallas kernels, on_device(): pl.pallas_call(functools.partial(pair_kernel, leaves, features), out_shap...  3.37 us

profile of v4, /device:TPU:72, one launch (start us, length us, event | category | flops | bytes accessed | tf_op | source)
XLA Modules:
  0.0 58.6 jit_solution(6646526958392938416)
XLA Ops:
  0.7 44.5 %upward.1 = (bf16[33,256,128]{2,1,0:T(8,128)(2,1)S(1)}, bf16[17,256,128]{2,1,0:T(8,128)(2,1)S(1)}, bf16[16,128,256]{2,1,0:T(8,128)(2,1)S(1)}, bf16[33,128,128]{2...) custom-call(bf16[16,64,256]{2,1,0:T(8,128)(2,1)} %points_in.1, ...), custom_call_target="tpu_custom_call" | custom-call | tf_op jit(solution)/shard_map/upward/pallas_call | solution.py:759
  45.1 3.4 %pairs.1 = (f32[16,16,256]{2,1,0:T(8,128)S(1)}, f32[16,16,128]{2,1,0:T(8,128)S(1)}, bf16[16,16,256]{2,1,0:T(8,128)(2,1)S(1)}, bf16[16,16,128]{2,1,0:T(8,128)(2,1)S(1)}) custom-call(s32[4,8,240]{2,1,0:T(8,128)S(4)} %get-tuple-element.29.queues, bf16[33,256,128]{2,1,0:T(8,128)(2,1)S(1)} %get-tuple-element.30.leaf_columns, ...), custom_call_target="tpu_custom_call" | custom-call | tf_op jit(solution)/shard_map/pairs/pallas_call | solution.py:837
  48.5 9.3 %returned.1 = f32[16,16,256]{2,1,0:T(8,128)S(1)} custom-call(f32[16,16,256]{2,1,0:T(8,128)S(1)} %get-tuple-element.42.near_own, f32[16,16,128]{2,1,0:T(8,128)S(1)} %get-tuple-element.43.far_leaf, bf16[16,16,256]{2,1,0:T(8,128)(2,1)S(1)} %get-tuple-element.44.near_out, bf16[16,16,128]{2,1,0:T(8,128)(2,1)S(1)} %get-tuple-element.45.far_out, ...), custom_call_target="tpu_custom_call" | custom-call | tf_op jit(solution)/shard_map/returned/pallas_call | solution.py:856
  57.9 0.7 %copy.16 = f32[16,16,256]{2,1,0:T(8,128)} copy(f32[16,16,256]{2,1,0:T(8,128)S(1)} %returned.1) | data formatting | bytes 524288
